TPU v7x, 256 devices: a whole 4x4x8 slice. The times are simulated.
256 devices in a mesh: dp: 2 (over z_hi), blk: 16 (over z_lo, x), head: 8 (over y, core).
Axes of the slice: x: 4, y: 4, z: 8 (z_hi: 2, z_lo: 4; z = z_hi * 4 + z_lo), core: 2. Of those that a mesh axis runs over, the one named last changes fastest.
Arguments:
- video_q: bfloat16 [2, 4096, 2048], P('dp', ('blk', 'head')), may hold values from -6 to 6
- video_k: bfloat16 [2, 4096, 2048], P('dp', ('blk', 'head')), may hold values from -6 to 6
- video_v: bfloat16 [2, 4096, 2048], P('dp', ('blk', 'head')), may hold values from -6 to 6
- video_out: bfloat16 [2, 4096, 2048], P('dp', ('blk', 'head')), may hold values from -6 to 6
- video_dout: bfloat16 [2, 4096, 2048], P('dp', ('blk', 'head')), may hold values from -48 to 48
- text_q: bfloat16 [2, 256, 2048], P('dp', 'head'), may hold values from -6 to 6
- text_k: bfloat16 [2, 256, 2048], P('dp', 'head'), may hold values from -6 to 6
- text_v: bfloat16 [2, 256, 2048], P('dp', 'head'), may hold values from -6 to 6
- text_out: bfloat16 [2, 256, 2048], P('dp', 'head'), may hold values from -6 to 6
- text_dout: bfloat16 [2, 256, 2048], P('dp', 'head'), may hold values from -48 to 48
- video_lse: float32 [2, 16, 4096], P('dp', 'head', 'blk'), may hold values from 7.5 to 9
- text_lse: float32 [2, 16, 256], P('dp', 'head'), may hold values from 7.5 to 9
- video_norm: bfloat16 [2, 4096, 3072], P('dp', ('blk', 'head')), may hold values from -24 to 24
- text_norm: bfloat16 [2, 256, 3072], P('dp', 'head'), may hold values from -6 to 6
- video_mod: float32 [2, 2, 3072], P('dp'), may hold values from -3 to 3
- text_mod: float32 [2, 2, 3072], P('dp'), may hold values from -3 to 3
- video_weight: bfloat16 [3072, 3, 2048], P(None, None, 'head'), may hold values from -0.109375 to 0.109375
- text_weight: bfloat16 [3072, 3, 2048], P(None, None, 'head'), may hold values from -0.109375 to 0.109375
Outputs:
- video_dnorm: bfloat16 [2, 4096, 3072], P('dp', ('blk', 'head'))
- text_dnorm: bfloat16 [2, 256, 3072], P('dp', 'head')
- video_wgrad: float32 [3072, 3, 2048], P(('dp', 'blk'), None, 'head')
- text_wgrad: float32 [3072, 3, 2048], P(('dp', 'blk'), None, 'head')
- video_mod_grad: float32 [2, 2, 3072], P('dp')
- text_mod_grad: float32 [2, 2, 3072], P('dp')
All inputs are finite; a program needn't handle non-finite values.
Results may differ from a plain program's by a relative error of at most 0.029.
Values may be sent and summed in bfloat16 or wider, within the bound.
A program may use at most 128 MiB of HBM per device.

v0:
```python
import jax
import jax.numpy as jnp
from jax import lax
from jax.sharding import PartitionSpec as P

D = 3072
DH = 128


def dot_rows(left, right):
    return lax.dot_general(
        left, right, (((1,), (1,)), ((), ())), preferred_element_type=jnp.float32
    )


def dot_cols(left, right):
    return lax.dot_general(
        left, right, (((0,), (0,)), ((), ())), preferred_element_type=jnp.float32
    )


def row_delta(dout, output, heads):
    products = dout.astype(jnp.float32) * output.astype(jnp.float32)
    return products.reshape(dout.shape[0], heads, DH).sum(axis=2)


def pair_grads(query, keys, values, dout, lse, delta):
    factor = DH ** (-0.5)
    heads = query.shape[1] // DH
    grads_q, grads_k, grads_v = ([], [], [])
    for head in range(heads):
        low = head * DH
        q_head = query[:, low : low + DH]
        k_head = keys[:, low : low + DH]
        v_head = values[:, low : low + DH]
        d_head = dout[:, low : low + DH]
        scores = dot_rows(q_head, k_head) * factor
        probs = jnp.exp(scores - lse[head][:, None])
        dprobs = dot_rows(d_head, v_head)
        dscores = (probs * (dprobs - delta[head][:, None])).astype(jnp.bfloat16)
        probs_b = probs.astype(jnp.bfloat16)
        grads_q.append(jnp.dot(dscores, k_head, preferred_element_type=jnp.float32) * factor)
        grads_k.append(dot_cols(dscores, q_head) * factor)
        grads_v.append(dot_cols(probs_b, d_head))
    return (
        jnp.concatenate(grads_q, axis=1),
        jnp.concatenate(grads_k, axis=1),
        jnp.concatenate(grads_v, axis=1),
    )


def body(
    video_q,
    video_k,
    video_v,
    video_out,
    video_dout,
    text_q,
    text_k,
    text_v,
    text_out,
    text_dout,
    video_lse,
    text_lse,
    video_norm,
    text_norm,
    video_mod,
    text_mod,
    video_weight,
    text_weight,
):
    head_q, head_k, head_v, head_out, head_dout, tq_all, tk_all, tv_all, tout_all, tdout_all = (
        lax.all_to_all(video_q[0], "head", split_axis=1, concat_axis=0, tiled=True),
        lax.all_to_all(video_k[0], "head", split_axis=1, concat_axis=0, tiled=True),
        lax.all_to_all(video_v[0], "head", split_axis=1, concat_axis=0, tiled=True),
        lax.all_to_all(video_out[0], "head", split_axis=1, concat_axis=0, tiled=True),
        lax.all_to_all(video_dout[0], "head", split_axis=1, concat_axis=0, tiled=True),
        lax.all_to_all(text_q[0], "head", split_axis=1, concat_axis=0, tiled=True),
        lax.all_to_all(text_k[0], "head", split_axis=1, concat_axis=0, tiled=True),
        lax.all_to_all(text_v[0], "head", split_axis=1, concat_axis=0, tiled=True),
        lax.all_to_all(text_out[0], "head", split_axis=1, concat_axis=0, tiled=True),
        lax.all_to_all(text_dout[0], "head", split_axis=1, concat_axis=0, tiled=True),
    )
    heads_here = head_q.shape[1] // DH
    video_delta = row_delta(head_dout, head_out, heads_here).T
    text_delta = row_delta(tdout_all, tout_all, heads_here).T
    video_lse_here = video_lse[0]
    text_lse_here = text_lse[0]
    step_q, step_k, step_v = pair_grads(
        head_q,
        lax.all_gather(head_k, "blk", axis=0, tiled=True),
        lax.all_gather(head_v, "blk", axis=0, tiled=True),
        head_dout,
        video_lse_here,
        video_delta,
    )
    key_buf = step_k
    value_buf = step_v
    video_gq, key_buf, value_buf = (step_q, key_buf, value_buf)
    video_gk, video_gv = (
        lax.psum_scatter(
            key_buf.astype(jnp.bfloat16), "blk", scatter_dimension=0, tiled=True
        ).astype(jnp.float32),
        lax.psum_scatter(
            value_buf.astype(jnp.bfloat16), "blk", scatter_dimension=0, tiled=True
        ).astype(jnp.float32),
    )
    from_text_q, text_k_part, text_v_part = pair_grads(
        head_q, tk_all, tv_all, head_dout, video_lse_here, video_delta
    )
    video_gq = video_gq + from_text_q
    text_q_part, video_k_extra, video_v_extra = pair_grads(
        tq_all, head_k, head_v, tdout_all, text_lse_here, text_delta
    )
    video_gk = video_gk + video_k_extra
    video_gv = video_gv + video_v_extra
    share = tq_all.shape[0] // lax.axis_size("blk")
    first = lax.axis_index("blk") * share
    share_q = lax.dynamic_slice_in_dim(tq_all, first, share, 0)
    share_dout = lax.dynamic_slice_in_dim(tdout_all, first, share, 0)
    share_lse = lax.dynamic_slice_in_dim(text_lse_here, first, share, 1)
    share_delta = lax.dynamic_slice_in_dim(text_delta, first, share, 1)
    rows_q, rows_k, rows_v = pair_grads(share_q, tk_all, tv_all, share_dout, share_lse, share_delta)
    text_q_part = text_q_part + lax.dynamic_update_slice_in_dim(
        jnp.zeros_like(text_q_part), rows_q, first, 0
    )
    text_gq, text_gk, text_gv = (
        lax.psum(text_q_part.astype(jnp.bfloat16), "blk").astype(jnp.float32),
        lax.psum((text_k_part + rows_k).astype(jnp.bfloat16), "blk").astype(jnp.float32),
        lax.psum((text_v_part + rows_v).astype(jnp.bfloat16), "blk").astype(jnp.float32),
    )
    video_grads = jnp.stack([video_gq, video_gk, video_gv], axis=1).astype(jnp.bfloat16)
    text_grads = jnp.stack([text_gq, text_gk, text_gv], axis=1).astype(jnp.bfloat16)
    part = video_grads
    video_back = lax.psum_scatter(
        jnp.einsum("rcf,dcf->rd", part, video_weight, preferred_element_type=jnp.float32).astype(
            jnp.bfloat16
        ),
        "head",
        scatter_dimension=0,
        tiled=True,
    ).astype(jnp.float32)
    part = text_grads
    text_back = lax.psum_scatter(
        jnp.einsum("rcf,dcf->rd", part, text_weight, preferred_element_type=jnp.float32).astype(
            jnp.bfloat16
        ),
        "head",
        scatter_dimension=0,
        tiled=True,
    ).astype(jnp.float32)
    video_gain = 1.0 + video_mod[0, 1]
    text_gain = 1.0 + text_mod[0, 1]
    video_nf = video_norm[0].astype(jnp.float32)
    text_nf = text_norm[0].astype(jnp.float32)
    video_dnorm = (video_gain * video_back).astype(jnp.bfloat16)
    text_dnorm = (text_gain * text_back).astype(jnp.bfloat16)
    video_stat = jnp.stack([jnp.sum(video_back, axis=0), jnp.sum(video_back * video_nf, axis=0)])
    text_stat = jnp.stack([jnp.sum(text_back, axis=0), jnp.sum(text_back * text_nf, axis=0)])
    video_total = lax.psum(video_stat, ("blk", "head"))
    text_total = lax.psum(text_stat, "head")
    gathered_norm = lax.all_gather(video_norm[0], "head", axis=0, tiled=True)
    video_in = (video_gain * gathered_norm.astype(jnp.float32) + video_mod[0, 0]).astype(
        jnp.bfloat16
    )
    groups = lax.axis_size("dp")
    blocks = lax.axis_size("blk")
    row_count = D // (groups * blocks)
    columns = video_in
    video_wgrad = lax.psum_scatter(
        jnp.einsum("rd,rcf->dcf", columns, video_grads, preferred_element_type=jnp.float32).astype(
            jnp.bfloat16
        ),
        ("dp", "blk"),
        scatter_dimension=0,
        tiled=True,
    ).astype(jnp.float32)
    text_rows_here = text_norm.shape[1]
    block_index = lax.axis_index("blk")
    norm_cols = lax.dynamic_index_in_dim(
        text_norm[0].reshape(text_rows_here, groups, blocks, row_count),
        block_index,
        2,
        keepdims=False,
    ).reshape(text_rows_here, groups * row_count)
    mod_cols = lax.dynamic_index_in_dim(
        text_mod[0].reshape(2, groups, blocks, row_count), block_index, 2, keepdims=False
    ).reshape(2, groups * row_count)
    gathered_text = lax.all_gather(norm_cols, "head", axis=0, tiled=True)
    text_in = ((1.0 + mod_cols[1]) * gathered_text.astype(jnp.float32) + mod_cols[0]).astype(
        jnp.bfloat16
    )
    columns = text_in
    text_wgrad = lax.psum_scatter(
        jnp.einsum("rd,rcf->dcf", columns, text_grads, preferred_element_type=jnp.float32).astype(
            jnp.bfloat16
        ),
        "dp",
        scatter_dimension=0,
        tiled=True,
    ).astype(jnp.float32)
    return (
        video_dnorm[None],
        text_dnorm[None],
        video_wgrad,
        text_wgrad,
        video_total[None],
        text_total[None],
    )


def solution(mesh):
    return jax.shard_map(
        body,
        mesh=mesh,
        in_specs=(
            P("dp", ("blk", "head"), None),
            P("dp", ("blk", "head"), None),
            P("dp", ("blk", "head"), None),
            P("dp", ("blk", "head"), None),
            P("dp", ("blk", "head"), None),
            P("dp", "head", None),
            P("dp", "head", None),
            P("dp", "head", None),
            P("dp", "head", None),
            P("dp", "head", None),
            P("dp", "head", "blk"),
            P("dp", "head", None),
            P("dp", ("blk", "head"), None),
            P("dp", "head", None),
            P("dp", None, None),
            P("dp", None, None),
            P(None, None, "head"),
            P(None, None, "head"),
        ),
        out_specs=(
            P("dp", ("blk", "head"), None),
            P("dp", "head", None),
            P(("dp", "blk"), None, "head"),
            P(("dp", "blk"), None, "head"),
            P("dp", None, None),
            P("dp", None, None),
        ),
        check_vma=False,
    )
```

profile of v0, /device:TPU:1, one launch (start us, length us, event | category | flops | bytes accessed | tf_op | source)
XLA Modules:
  0.0 1296.5 jit_solution(3308002840247604128)
XLA Ops:
  9.2 11.7 all_to_all.178
  22.6 4.1 all-to-all-start.4
  29.1 2.9 all-to-all-done.4
  32.0 4.1 all-to-all-start.7
  36.2 5.3 all-to-all-done.7
  41.5 4.1 all-to-all-start.9
  51.3 3.7 all-to-all-start.8
  55.0 5.7 all-to-all-done.8
  60.7 3.7 all-to-all-start.5
  65.0 5.2 all-to-all-done.5
  70.2 3.7 all-to-all-start.2
  74.0 5.2 all-to-all-done.2
  79.2 4.1 all-to-all-start.6
  84.1 4.6 all-to-all-done.6
  88.6 4.1 all-to-all-start.3
  93.9 4.1 all-to-all-done.3
  98.1 4.1 all-to-all-start
  112.1 2.0 copy-done.2
  120.5 60.8 %all-gather.7.cloned.1.call-done = bf16[4096,256]{1,0:T(8,128)(2,1)} async-done(((bf16[256,256]{1,0:T(8,128)(2,1)}), bf16[4096,256]{1,0:T(8,128)(2,1)}) %all-gather.7.cloned.1.call-update) | async-done | bytes 2097168 | tf_op jit(solution)/shard_map/all_gather | solution.py:92
  181.3 3.4 fusion.6
  193.7 23.5 %all_gather.15 = bf16[256,192]{1,0:T(8,128)(2,1)S(1)} all-gather(bf16[32,192]{1,0:T(8,128)(2,1)S(1)} %reshape.178), channel_id=1, replica_groups=mesh['dp'=2,'blk'=16,'head'=8] {'head'}, dimensions={0}, use_global_device_ids=true | all-gather | bytes 110592 | tf_op jit(solution)/shard_map/all_gather | solution.py:189
  217.2 125.6 %all-reduce.3.cloned.1.call-done = (bf16[256,1,256]{0,2,1:T(8,128)(2,1)}, bf16[256,1,256]{0,2,1:T(8,128)(2,1)}, bf16[256,1,256]{0,2,1:T(8,128)(2,1)}) async-done(((bf16[256,1,256]{0,2,1:T(8,128)(2,1)}, bf16[256,1,256]{0,2,1:T(8,128)(2,1)}, bf16[256,1,256]{0,2,1:T(8,128)(2,1)}), (bf16[256,1,256]{0,2,1:T(8,128)(2,1)}, bf16[256,1,256]{0,2,1:T(8,128)(2,1)}, ...) | async-done | bytes 393232 | tf_op jit(solution)/shard_map/psum | solution.py:128
  347.5 5.1 fusion.11
  356.2 75.6 %reduce-scatter.9.cloned.1.call-done = bf16[256,256]{0,1:T(8,128)(2,1)} async-done(((bf16[4096,256]{0,1:T(8,128)(2,1)}), bf16[256,256]{0,1:T(8,128)(2,1)}) %reduce-scatter.9.cloned.1.call-update) | async-done | bytes 131088 | tf_op jit(solution)/shard_map/reduce_scatter | solution.py:104
  432.8 85.8 %reduce-scatter.7.cloned.1.call-done = bf16[256,256]{0,1:T(8,128)(2,1)} async-done(((bf16[4096,256]{0,1:T(8,128)(2,1)}), bf16[256,256]{0,1:T(8,128)(2,1)}) %reduce-scatter.7.cloned.1.call-update) | async-done | bytes 131088 | tf_op jit(solution)/shard_map/reduce_scatter | solution.py:101
  519.5 5.0 fusion.10
  524.7 5.0 convolution_convert_fusion
  530.4 22.0 %reduce-scatter.17.cloned.1.call-done = bf16[96,3,256]{2,0,1:T(8,128)(2,1)} async-done(((bf16[192,3,256]{2,0,1:T(8,128)(2,1)}), bf16[96,3,256]{2,0,1:T(8,128)(2,1)}) %reduce-scatter.17.cloned.1.call-update) | async-done | bytes 147472 | tf_op jit(solution)/shard_map/reduce_scatter | solution.py:194
  554.1 30.3 %reduce-scatter.13.cloned.1.call-done = bf16[32,3072]{1,0:T(8,128)(2,1)} async-done(((bf16[256,3072]{1,0:T(8,128)(2,1)}), bf16[32,3072]{1,0:T(8,128)(2,1)}) %reduce-scatter.13.cloned.1.call-update) | async-done | bytes 196624 | tf_op jit(solution)/shard_map/reduce_scatter | solution.py:144
  586.1 24.3 %psum.39 = f32[1,2,3072]{2,1,0:T(2,128)} all-reduce(f32[1,2,3072]{2,1,0:T(2,128)S(1)} %maximum_bitcast_fusion.1), channel_id=1, replica_groups=mesh['dp'=2,'blk'=16,'head'=8] {'head'}, use_global_device_ids=true, to_apply=%region_16.17 | all-reduce | flops 6144 | bytes 49152 | tf_op jit(solution)/shard_map/psum | solution.py:161
  610.4 10.8 reduce-scatter.11.cloned.1.call-done
  622.9 664.9 %psum.38 = f32[1,2,3072]{2,1,0:T(2,128)} all-reduce(f32[1,2,3072]{2,1,0:T(2,128)S(1)} %maximum_bitcast_fusion), channel_id=1, replica_groups=mesh['dp'=2,'blk'=16,'head'=8] {'blk','head'}, use_global_device_ids=true, to_apply=%region_13.0 | all-reduce | flops 6144 | bytes 49152 | tf_op jit(solution)/shard_map/psum | solution.py:160
  (190 shorter events, 55.9 us)
Async XLA Ops:
  8.0 20.4 %copy-start.19 = (bf16[1,32,2048]{2,1,0:T(8,128)(2,1)S(1)}, bf16[1,32,2048]{2,1,0:T(8,128)(2,1)}, u32[]{:S(2)}) copy-start(bf16[1,32,2048]{2,1,0:T(8,128)(2,1)} %param.26) | copy-start | bytes 393220
  8.0 28.2 %copy-start.30 = (f32[1,2,256]{2,1,0:T(2,128)S(1)}, f32[1,2,256]{2,1,0:T(2,128)}, u32[]{:S(2)}) copy-start(f32[1,2,256]{2,1,0:T(2,128)} %param.28) | copy-start | bytes 6148
  8.0 37.6 %copy-start.29 = (f32[1,2,256]{2,1,0:T(2,128)S(1)}, f32[1,2,256]{2,1,0:T(2,128)}, u32[]{:S(2)}) copy-start(f32[1,2,256]{2,1,0:T(2,128)} %param.29) | copy-start | bytes 6148
  8.0 37.6 %copy-start.20 = (bf16[1,32,2048]{2,1,0:T(8,128)(2,1)S(1)}, bf16[1,32,2048]{2,1,0:T(8,128)(2,1)}, u32[]{:S(2)}) copy-start(bf16[1,32,2048]{2,1,0:T(8,128)(2,1)} %param.18) | copy-start | bytes 393220
  8.0 38.3 %copy-start.21 = (bf16[1,32,2048]{2,1,0:T(8,128)(2,1)S(1)}, bf16[1,32,2048]{2,1,0:T(8,128)(2,1)}, u32[]{:S(2)}) copy-start(bf16[1,32,2048]{2,1,0:T(8,128)(2,1)} %param.20) | copy-start | bytes 393220
  8.1 102.1 %all-gather.5.cloned.1.call-start = ((), (), s32[]{:S(2)}) async-start(), calls=%async_computation.16 | async-start | bytes 2228224 | tf_op jit(solution)/shard_map/all_gather | solution.py:91
  9.2 37.9 %copy-start.22 = (bf16[1,32,2048]{2,1,0:T(8,128)(2,1)S(1)}, bf16[1,32,2048]{2,1,0:T(8,128)(2,1)}, u32[]{:S(2)}) copy-start(bf16[1,32,2048]{2,1,0:T(8,128)(2,1)} %param.22) | copy-start | bytes 393220
  20.9 26.9 %copy-start.23 = (bf16[1,32,2048]{2,1,0:T(8,128)(2,1)S(1)}, bf16[1,32,2048]{2,1,0:T(8,128)(2,1)}, u32[]{:S(2)}) copy-start(bf16[1,32,2048]{2,1,0:T(8,128)(2,1)} %param.24) | copy-start | bytes 393220
  21.9 26.6 %copy-start.24 = (bf16[1,32,2048]{2,1,0:T(8,128)(2,1)S(1)}, bf16[1,32,2048]{2,1,0:T(8,128)(2,1)}, u32[]{:S(2)}) copy-start(bf16[1,32,2048]{2,1,0:T(8,128)(2,1)} %param.25) | copy-start | bytes 393220
  22.6 9.4 all-to-all-start.4
  26.7 22.5 %copy-start.25 = (bf16[1,32,2048]{2,1,0:T(8,128)(2,1)S(1)}, bf16[1,32,2048]{2,1,0:T(8,128)(2,1)}, u32[]{:S(2)}) copy-start(bf16[1,32,2048]{2,1,0:T(8,128)(2,1)} %param.27) | copy-start | bytes 393220
  32.0 9.4 all-to-all-start.7
  41.5 9.8 all-to-all-start.9
  51.3 9.4 all-to-all-start.8
  60.7 9.4 all-to-all-start.5
  64.5 29.0 %copy-start.7 = (bf16[32,8,256]{2,0,1:T(8,128)(2,1)S(1)}, bf16[32,8,256]{2,0,1:T(8,128)(2,1)}, u32[]{:S(2)}) copy-start(bf16[32,8,256]{2,0,1:T(8,128)(2,1)} %all_to_all.178) | copy-start | bytes 393220
  70.2 9.0 all-to-all-start.2
  79.2 9.4 all-to-all-start.6
  88.6 9.4 all-to-all-start.3
  98.1 9.4 all-to-all-start
  102.2 79.1 %all-gather.7.cloned.1.call-start = ((), (), s32[]{:S(2)}) async-start(), calls=%async_computation.17 | async-start | bytes 2228224 | tf_op jit(solution)/shard_map/all_gather | solution.py:92
  102.9 239.9 %all-reduce.3.cloned.1.call-start = ((), (), s32[]{:S(2)}) async-start(), calls=%async_computation.25 | async-start | bytes 786432 | tf_op jit(solution)/shard_map/psum | solution.py:128
  110.0 321.8 %reduce-scatter.9.cloned.1.call-start = ((), (), s32[]{:S(2)}) async-start(), calls=%async_computation.19 | async-start | bytes 2228224 | tf_op jit(solution)/shard_map/reduce_scatter | solution.py:104
  120.5 398.1 %reduce-scatter.7.cloned.1.call-start = ((), (), s32[]{:S(2)}) async-start(), calls=%async_computation.18 | async-start | bytes 2228224 | tf_op jit(solution)/shard_map/reduce_scatter | solution.py:101
  190.5 334.2 %all-gather.9.cloned.1.call-start = ((), (), s32[]{:S(2)}) async-start(), calls=%async_computation.24 | async-start | bytes 1769472 | tf_op jit(solution)/shard_map/all_gather | solution.py:162
  191.1 361.4 %reduce-scatter.17.cloned.1.call-start = ((), (), s32[]{:S(2)}) async-start(), calls=%async_computation.23 | async-start | bytes 442368 | tf_op jit(solution)/shard_map/reduce_scatter | solution.py:194
  347.4 5.5 copy-start.12
  347.4 236.9 %reduce-scatter.13.cloned.1.call-start = ((), (), s32[]{:S(2)}) async-start(), calls=%async_computation.21 | async-start | bytes 1769472 | tf_op jit(solution)/shard_map/reduce_scatter | solution.py:144
  352.6 268.6 %reduce-scatter.11.cloned.1.call-start = ((), (), s32[]{:S(2)}) async-start(), calls=%async_computation.20 | async-start | bytes 1769472 | tf_op jit(solution)/shard_map/reduce_scatter | solution.py:135
  524.6 763.2 %reduce-scatter.15.cloned.1.call-start = ((), (), s32[]{:S(2)}) async-start(), calls=%async_computation.22 | async-start | bytes 4866048 | tf_op jit(solution)/shard_map/reduce_scatter | solution.py:170
  529.7 54.7 %copy-start.15 = (bf16[1,32,3072]{2,1,0:T(8,128)(2,1)S(1)}, bf16[1,32,3072]{2,1,0:T(8,128)(2,1)}, u32[]{:S(2)}) copy-start(bf16[1,32,3072]{2,1,0:T(8,128)(2,1)} %param.31) | copy-start | bytes 589828
  529.7 91.5 %copy-start.16 = (bf16[1,32,3072]{2,1,0:T(8,128)(2,1)S(1)}, bf16[1,32,3072]{2,1,0:T(8,128)(2,1)}, u32[]{:S(2)}) copy-start(bf16[1,32,3072]{2,1,0:T(8,128)(2,1)} %param.30) | copy-start | bytes 589828
  (18 other events, 42.9 us)
Sparse Core Ops, SparseCore 0:
  21.0 74.1 all-gather.4
  105.4 75.8 all-gather.6
  184.1 158.7 all-reduce.2
  345.4 86.3 reduce-scatter.8
  434.4 84.1 reduce-scatter.6
  521.6 30.7 reduce-scatter.16
  555.1 29.1 reduce-scatter.12
  587.1 34.0 reduce-scatter.10
  625.6 222.0 reduce-scatter.14
Sparse Core Ops, SparseCore 1:
  192.9 35.2 all-gather.8
where the time goes:
time: 1300 us
  blocking collectives  724 us (56%)
  waiting for transfers between devices  447 us (34%)
  starting transfers between devices  36.6 us (3%)
  matrix products  34.2 us (3%)
  local copies, waits for them, and re-layouts  25.3 us (2%)
  between operations  16 us (1%)
  other arithmetic  13.4 us (1%)
    psum x1, blocking collectives, body(): video_total = lax.psum(video_stat, ('blk', 'head'))  665 us
    psum x1, waiting for transfers between devices, body(): lax.psum(text_q_part.astype(jnp.bfloat16), 'blk').astype(jnp.float32)  126 us
    reduce_scatter x1, waiting for transfers between devices, body(): lax.psum_scatter(key_buf.astype(jnp.bfloat16), 'blk', scatter_dimension=0...  85.8 us
    reduce_scatter x1, waiting for transfers between devices, body(): lax.psum_scatter(value_buf.astype(jnp.bfloat16), 'blk', scatter_dimension...  75.6 us
    all_gather x1, waiting for transfers between devices, body(): lax.all_gather(head_v, 'blk', axis=0, tiled=True)  60.8 us
    reduce_scatter x1, waiting for transfers between devices, body(): lax.psum_scatter(jnp.einsum('rcf,dcf->rd', part, text_weight, preferred_e...  30.3 us
  transfers between devices with their start and end apart: 19, of which 16 were waited for; matrix products, arithmetic and copies ran while one was open for 5% of the time, Pallas kernels for 0%

commit v1 on v0

v1 whole, which is shorter than its diff:
```python
import functools

import jax
import jax.numpy as jnp
from jax import lax
from jax.experimental import pallas as pl
from jax.experimental.pallas import tpu as pltpu
from jax.sharding import PartitionSpec as P

MESH = pl.DeviceIdType.MESH
D = 3072
DH = 128
SET = 512
ROWS = 544
TXT = 32
FACTOR = DH ** (-0.5)
LOG2E = 1.4426950408889634
F32 = jnp.float32
BF16 = jnp.bfloat16

NAMES = (
    "a_q", "a_d", "a_k", "a_v", "a_st", "a_lse", "a_tq", "a_td", "a_tk", "a_tv",
    "b_kv", "b_qc", "b_sc", "b_qz", "b_sz", "b_qf", "b_sf", "vin", "tin",
    "d_kv", "d_qc", "d_qz", "e0", "e1", "e2", "tz", "te", "w0", "w1", "w2",
    "bc", "by", "tr", "tdn", "ts", "tsx", "s1", "s2", "s3", "s4", "tw",
)
SEM = {name: index for index, name in enumerate(NAMES)}
LOCALS = ("out", "dout", "tout", "tdout", "nrm", "tnrm", "w", "tw", "lse", "tlse", "mod", "tmod")


def nt(left, right):
    return lax.dot_general(left, right, (((1,), (1,)), ((), ())), preferred_element_type=F32)


def tn(left, right):
    return lax.dot_general(left, right, (((0,), (0,)), ((), ())), preferred_element_type=F32)


def nn(left, right):
    return jnp.dot(left, right, preferred_element_type=F32)


def kernel(
    q, k, v, out, dout, tq, tk, tv, tout, tdout, lse, tlse, norm, tnorm, mod, tmod, weight, tweight,
    o_dn, o_tdn, o_wg, o_twg, o_vs, o_ts,
    l_out, l_dout, l_tout, l_tdout, l_nrm, l_tnrm, l_w, l_tw, l_lse, l_tlse, l_mod, l_tmod,
    qd, kv, st, d_send, d_recv, l_send, l_recv,
    gk_acc, gv_acc, gq_acc, dkv_s, dkv_r, dqc_s, dqc_r, dqz_s, dqz_r, g_fin,
    vin_s, vin_all, tin_s, tin_all, gr, tz, tg, gs,
    w_send, w_recv, w_own, b_send, b_recv, b_own, y_send, y_recv,
    t_tmp, tr_send, tr_recv, tdn_all, ts_buf, tsx_buf, s1_s, s1_r, s2_buf, s3_buf, s4_buf, tw_s, tw_r,
    rs, ss, ls,
):
    dp = lax.axis_index("dp")
    blk = lax.axis_index("blk")
    head = lax.axis_index("head")
    z, x, y, c = blk // 4, blk % 4, head // 2, head % 2
    me = y * 4 + x
    mine = x // 2
    half = x % 2

    def dev(dz=None, dx=None, dy=None, dc=None, ddp=None):
        zz = z if dz is None else dz
        xx = x if dx is None else dx
        yy = y if dy is None else dy
        cc = c if dc is None else dc
        return {"dp": dp if ddp is None else ddp, "blk": zz * 4 + xx, "head": yy * 2 + cc}

    def remote(src, dst, name, to):
        return pltpu.make_async_remote_copy(
            src_ref=src, dst_ref=dst, send_sem=ss.at[SEM[name]], recv_sem=rs.at[SEM[name]],
            device_id=to, device_id_type=MESH)

    def local(src, dst, name):
        return pltpu.make_async_copy(src, dst, rs.at[SEM[name]])

    def got(ref, name):
        pltpu.make_async_copy(ref, ref, rs.at[SEM[name]]).wait()

    def sent(ref, name):
        pltpu.make_async_copy(ref, ref, ss.at[SEM[name]]).wait()

    def rows32(index):
        return pl.ds(pl.multiple_of(index * 32, 32), 32)

    def lanes(index, width=128):
        return pl.ds(pl.multiple_of(index * width, 128), width)

    def send_a(t, carry):
        to = dev(dx=t % 4, dy=t // 4)
        for src, dst, name in ((k, kv.at[0, 0], "a_k"), (v, kv.at[0, 1], "a_v"),
                               (q, qd.at[0, 0], "a_q"), (dout, qd.at[0, 1], "a_d")):
            piece = src.at[:, lanes(t)]
            place = dst.at[rows32(me)]

            @pl.when(t != me)
            def _():
                remote(piece, place, name, to).start()

            @pl.when(t == me)
            def _():
                local(piece, place, name).start()
        return carry

    lax.fori_loop(0, 16, send_a, 0)

    @pl.when(y == z)
    def _():
        for t in range(4):
            for src, dst, name in ((tk, kv.at[0, 0], "a_tk"), (tv, kv.at[0, 1], "a_tv"),
                                   (tq, qd.at[0, 0], "a_tq"), (tdout, qd.at[0, 1], "a_td")):
                piece = src.at[:, lanes(4 * t + x)]
                place = dst.at[pl.ds(SET, TXT)]

                @pl.when(t != y)
                def _():
                    remote(piece, place, name, dev(dy=t)).start()

                @pl.when(t == y)
                def _():
                    local(piece, place, name).start()

    loads = {
        "out": (out, l_out), "dout": (dout, l_dout), "tout": (tout, l_tout), "tdout": (tdout, l_tdout),
        "nrm": (norm, l_nrm), "tnrm": (tnorm, l_tnrm), "lse": (lse, l_lse), "tlse": (tlse, l_tlse),
        "mod": (mod, l_mod), "tmod": (tmod, l_tmod), "w": (weight, l_w),
        "tw": (tweight.at[:, pl.ds(pl.multiple_of(x * 768, 768), 768), :], l_tw),
    }
    copies = {n: pltpu.make_async_copy(s, d, ls.at[LOCALS.index(n)]) for n, (s, d) in loads.items()}
    for name in ("out", "dout", "lse", "tlse", "tout", "tdout", "nrm", "mod", "tnrm", "tmod", "w", "tw"):
        copies[name].start()

    lane = lax.broadcasted_iota(jnp.int32, (16, 128), 1)
    ones = jnp.where(
        lax.broadcasted_iota(jnp.int32, (16, 2048), 1) // DH
        == lax.broadcasted_iota(jnp.int32, (16, 2048), 0), 1.0, 0.0).astype(BF16)

    def delta_rows(a_ref, b_ref):
        total = jnp.zeros((16, 128), F32)
        products = a_ref[...].astype(F32) * b_ref[...].astype(F32)
        high = products.astype(BF16)
        low = (products - high.astype(F32)).astype(BF16)
        for part in (high, low):
            total = total + nt(ones, jnp.concatenate([part] * 4, axis=0))
        return total

    copies["out"].wait()
    copies["dout"].wait()
    video_delta = jnp.where(lane // 32 == x, delta_rows(l_out, l_dout), 0.0)
    copies["tout"].wait()
    copies["tdout"].wait()
    text_delta = jnp.where(lane < 32, delta_rows(l_tout, l_tdout), 0.0)
    d_send[...] = jnp.zeros_like(d_send)
    for h in range(16):
        d_send[h, 0:1, :] = video_delta[h:h + 1, :]
        d_send[h, 1:2, :] = text_delta[h:h + 1, :]

    def send_delta(t, carry):
        @pl.when(t != me)
        def _():
            remote(d_send.at[t], d_recv.at[me], "a_st", dev(dx=t % 4, dy=t // 4)).start()

        @pl.when(t == me)
        def _():
            local(d_send.at[t], d_recv.at[me], "a_st").start()
        return carry

    lax.fori_loop(0, 16, send_delta, 0)

    copies["lse"].wait()
    copies["tlse"].wait()
    lane8 = lax.broadcasted_iota(jnp.int32, (8, 128), 1)
    l_send[...] = jnp.zeros_like(l_send)
    for j in range(2):
        for cc in range(2):
            for yy in range(4):
                row = jnp.broadcast_to(l_lse[j:j + 1, 128 * (yy // 2):128 * (yy // 2) + 128], (8, 128))
                shift = (32 * x + 256 - (yy % 2) * 64 - cc * 32) % 128
                row = jnp.where(lane8 // 32 == x, pltpu.roll(row, shift, 1), 0.0)
                l_send[j, cc, yy:yy + 1, :] = row[0:1, :]
            row = jnp.broadcast_to(l_tlse[j:j + 1, pl.ds(pl.multiple_of((z // 2) * 128, 128), 128)], (8, 128))
            shift = (256 - (z % 2) * 64 - cc * 32) % 128
            row = jnp.where(lane8 < 32, pltpu.roll(row, shift, 1), 0.0)
            l_send[j, cc, 4:5, :] = row[0:1, :]
    for j in range(2):
        for cc in range(2):
            own = jnp.logical_and(x == 2 * c + j, c == cc)

            @pl.when(jnp.logical_not(own))
            def _():
                remote(l_send.at[j, cc], l_recv.at[x], "a_lse", dev(dx=2 * c + j, dc=cc)).start()

            @pl.when(own)
            def _():
                local(l_send.at[j, cc], l_recv.at[x], "a_lse").start()

    copies["nrm"].wait()
    copies["mod"].wait()
    gain = 1.0 + l_mod[1:2, :]
    vin = (gain * l_nrm[...].astype(F32) + l_mod[0:1, :])
    for xx in range(4):
        parts = [vin[:, 384 * m + 96 * xx:384 * m + 96 * xx + 96] for m in range(8)]
        vin_s[xx] = jnp.concatenate(parts, axis=1).astype(BF16)
    copies["tnrm"].wait()
    copies["tmod"].wait()
    tgain = 1.0 + l_tmod[1:2, :]
    tin_s[...] = (tgain * l_tnrm[...].astype(F32) + l_tmod[0:1, :]).astype(BF16)

    gk_acc[...] = jnp.zeros_like(gk_acc)
    gv_acc[...] = jnp.zeros_like(gv_acc)
    gq_acc[...] = jnp.zeros_like(gq_acc)

    got(kv.at[0, 0, pl.ds(0, SET)], "a_k")
    got(kv.at[0, 1, pl.ds(0, SET)], "a_v")
    got(kv.at[0, 0, pl.ds(SET, TXT)], "a_tk")
    got(kv.at[0, 1, pl.ds(SET, TXT)], "a_tv")
    zn = z + 1 - 2 * (z % 2)
    zf = (z + 2) % 4
    remote(kv.at[0], kv.at[1], "b_kv", dev(dz=zn)).start()
    got(qd.at[0, 0, pl.ds(0, SET)], "a_q")
    got(qd.at[0, 1, pl.ds(0, SET)], "a_d")
    got(qd.at[0, 0, pl.ds(SET, TXT)], "a_tq")
    got(qd.at[0, 1, pl.ds(SET, TXT)], "a_td")
    remote(qd.at[0], qd.at[1], "b_qz", dev(dz=zf)).start()
    remote(qd.at[0], qd.at[2], "b_qc", dev(dc=1 - c)).start()
    got(d_recv, "a_st")
    got(l_recv, "a_lse")
    for yy in range(4):
        st[0, yy:yy + 1, :] = LOG2E * (l_recv[0, yy:yy + 1, :] + l_recv[1, yy:yy + 1, :]
                                       + l_recv[2, yy:yy + 1, :] + l_recv[3, yy:yy + 1, :])
        st[0, 4 + yy:5 + yy, :] = (d_recv[4 * yy, 0:1, :] + d_recv[4 * yy + 1, 0:1, :]
                                   + d_recv[4 * yy + 2, 0:1, :] + d_recv[4 * yy + 3, 0:1, :])
    st[0, 8:9, :] = LOG2E * l_recv[0, 4:5, :]
    st[0, 9:10, :] = d_recv[z * 4 + x, 1:2, :]
    st[0, 10:16, :] = jnp.zeros((6, 128), F32)
    remote(st.at[0], st.at[1], "b_sz", dev(dz=zf)).start()
    remote(st.at[0], st.at[2], "b_sc", dev(dc=1 - c)).start()

    def send_vin(t, carry):
        hd, xx = t // 4, t % 4
        place = vin_all.at[pl.ds(pl.multiple_of(c * SET + me * 32, 32), 32)]
        own = jnp.logical_and(hd == head, xx == x)

        @pl.when(jnp.logical_not(own))
        def _():
            remote(vin_s.at[xx], place, "vin", dev(dx=xx, dy=hd // 2, dc=hd % 2)).start()

        @pl.when(own)
        def _():
            local(vin_s.at[xx], place, "vin").start()
        return carry

    lax.fori_loop(0, 32, send_vin, 0)

    window = jnp.minimum((blk * 96) // 128 * 128, 1280)

    def send_tin(hd, carry):
        for other in range(2):
            piece = tin_s.at[:, pl.ds(pl.multiple_of(other * 1536 + window, 128), 256)]
            place = tin_all.at[rows32(head), pl.ds(other * 256, 256)]

            @pl.when(hd != head)
            def _():
                remote(piece, place, "tin", dev(dy=hd // 2, dc=hd % 2)).start()

            @pl.when(hd == head)
            def _():
                local(piece, place, "tin").start()
        return carry

    lax.fori_loop(0, 8, send_tin, 0)

    def pair(lse_row, delta_row, query, dquery, keys, values):
        probs = jnp.exp2(nt(keys, query) * (FACTOR * LOG2E) - lse_row)
        dscores = (probs * (nt(values, dquery) - delta_row)).astype(BF16)
        return probs.astype(BF16), dscores

    def row512(i, first):
        return jnp.concatenate([st[i, first + n:first + n + 1, :] for n in range(4)], axis=1)

    def attend(step, carry):
        i = (step % 2) * 2 + step // 4
        j = ((step + 2) // 4) % 2

        @pl.when(step == 1)
        def _():
            got(qd.at[2], "b_qc")
            got(st.at[2], "b_sc")

        @pl.when(step == 2)
        def _():
            got(kv.at[1], "b_kv")

        @pl.when(step == 4)
        def _():
            got(qd.at[1], "b_qz")
            remote(qd.at[1], qd.at[3], "b_qf", dev(dc=1 - c)).start()
            got(st.at[1], "b_sz")
            remote(st.at[1], st.at[3], "b_sf", dev(dc=1 - c)).start()

        @pl.when(step == 5)
        def _():
            got(qd.at[3], "b_qf")
            got(st.at[3], "b_sf")

        query, dquery = qd[i, 0, 0:SET, :], qd[i, 1, 0:SET, :]
        keys, values = kv[j, 0], kv[j, 1]
        probs, dscores = pair(row512(i, 0), row512(i, 4), query, dquery, keys, values)
        gv_acc[j] += nn(probs, dquery)
        gk_acc[j] += nn(dscores, query)
        gq_acc[i, 0:SET, :] += tn(dscores, keys)
        return carry

    def attend_text(j):
        query = jnp.concatenate([qd[i, 0, SET:ROWS, :] for i in range(4)], axis=0)
        dquery = jnp.concatenate([qd[i, 1, SET:ROWS, :] for i in range(4)], axis=0)
        lse_row = jnp.zeros((8, 128), F32)
        delta_row = jnp.zeros((8, 128), F32)
        for i in range(4):
            one, two = (jnp.broadcast_to(st[i, r:r + 1, :], (8, 128)) for r in (8, 9))
            lse_row = lse_row + (pltpu.roll(one, 32 * i, 1) if i else one)
            delta_row = delta_row + (pltpu.roll(two, 32 * i, 1) if i else two)
        keys, values = kv[j, 0], kv[j, 1]
        probs, dscores = pair(lse_row[0:1, :], delta_row[0:1, :], query, dquery, keys, values)
        gv_acc[j] += nn(probs, dquery)
        gk_acc[j] += nn(dscores, query)
        from_text = tn(dscores, keys)
        for i in range(4):
            gq_acc[i, SET:ROWS, :] += from_text[32 * i:32 * i + 32, :]

    lax.fori_loop(0, 6, attend, 0)
    attend_text(1)
    dkv_s[0] = (gk_acc[1] * FACTOR).astype(BF16)
    dkv_s[1] = gv_acc[1].astype(BF16)
    remote(dkv_s, dkv_r, "d_kv", dev(dz=zn)).start()
    lax.fori_loop(6, 8, attend, 0)
    attend_text(0)
    dqc_s[0] = (gq_acc[2] * FACTOR).astype(BF16)
    dqc_s[1] = (gq_acc[3] * FACTOR).astype(BF16)
    remote(dqc_s, dqc_r, "d_qc", dev(dc=1 - c)).start()
    got(dqc_r, "d_qc")
    dqz_s[...] = (gq_acc[1] * FACTOR + dqc_r[1].astype(F32)).astype(BF16)
    remote(dqz_s, dqz_r, "d_qz", dev(dz=zf)).start()

    def send_grads(ch):
        for xx in range(4):
            own = jnp.logical_and(x == xx, c == mine)
            piece = g_fin.at[ch, pl.ds(0, SET)]
            place = gr.at[ch, pl.ds(pl.multiple_of(c * SET, SET), SET), lanes(half)]

            @pl.when(jnp.logical_not(own))
            def _():
                remote(piece, place, "e%d" % ch, dev(dx=xx, dc=mine)).start()

            @pl.when(own)
            def _():
                local(piece, place, "e%d" % ch).start()

    got(dkv_r, "d_kv")
    g_fin[1] = (gk_acc[0] * FACTOR + dkv_r[0].astype(F32)).astype(BF16)
    send_grads(1)
    g_fin[2] = (gv_acc[0] + dkv_r[1].astype(F32)).astype(BF16)
    send_grads(2)
    got(dqz_r, "d_qz")
    g_fin[0] = (gq_acc[0] * FACTOR + dqc_r[0].astype(F32) + dqz_r[...].astype(F32)).astype(BF16)
    send_grads(0)

    for zz in range(4):
        piece = g_fin.at[:, pl.ds(SET, TXT)]

        @pl.when(z != zz)
        def _():
            remote(piece, tz.at[:, z], "tz", dev(dz=zz)).start()

        @pl.when(z == zz)
        def _():
            local(piece, tz.at[:, z], "tz").start()
    got(tz, "tz")
    for xx in range(4):
        own = jnp.logical_and(x == xx, c == mine)
        place = tg.at[:, :, c, :, lanes(half)]

        @pl.when(jnp.logical_not(own))
        def _():
            remote(tz, place, "te", dev(dx=xx, dc=mine)).start()

        @pl.when(own)
        def _():
            local(tz, place, "te").start()

    pos = dp * 4 + z
    got(vin_all, "vin")
    for ch in (1, 2, 0):
        got(gr.at[ch], "e%d" % ch)
        grads = gr[ch]
        for other in range(8):
            if other % 4 == 0:
                term = tn(vin_all[:, 96 * other:96 * other + 384], grads)
            piece = term[96 * (other % 4):96 * (other % 4) + 96, :]
            w_send[other, ch] = piece.astype(BF16)

            @pl.when(pos != other)
            def _():
                remote(w_send.at[other, ch], w_recv.at[pos, ch], "w%d" % ch,
                       dev(ddp=other // 4, dz=other % 4)).start()

            @pl.when(pos == other)
            def _():
                w_own[ch] = piece

    for ch in range(3):
        for cc in range(2):
            for yy in range(4):
                first = pl.multiple_of(cc * SET + (yy * 4 + x) * 32, 32)
                gs[ch, cc * 128 + yy * 32:cc * 128 + yy * 32 + 32, :] = gr[ch, pl.ds(first, 32), :]
    copies["w"].wait()
    for n in range(6):
        cols = slice(512 * n, 512 * n + 512)
        term = (nt(gs[0], l_w[0, cols, :]) + nt(gs[1], l_w[1, cols, :]) + nt(gs[2], l_w[2, cols, :]))

        @pl.when(c == 0)
        def _():
            b_own[:, cols] = term[0:128, :]
            b_send[:, cols] = term[128:256, :].astype(BF16)

        @pl.when(c == 1)
        def _():
            b_own[:, cols] = term[128:256, :]
            b_send[:, cols] = term[0:128, :].astype(BF16)
    remote(b_send, b_recv, "bc", dev(dc=1 - c)).start()

    got(tg, "te")
    got(tin_all, "tin")
    first = pl.multiple_of(blk * 96 - window, 32)
    for ch in range(3):
        grads = tg[ch].reshape(256, 256)
        term = tn(tin_all[...], grads)
        t_tmp[...] = term.astype(BF16)
        away = pl.multiple_of((1 - dp) * 256 + first, 32)
        near = pl.multiple_of(dp * 256 + first, 32)
        tw_s[ch] = t_tmp[pl.ds(away, 96), :]
        o_twg[ch] = t_tmp[pl.ds(near, 96), :].astype(F32)
    remote(tw_s, tw_r, "tw", dev(ddp=1 - dp)).start()
    copies["tw"].wait()
    term = (nt(tg[0].reshape(256, 256), l_tw[0]) + nt(tg[1].reshape(256, 256), l_tw[1])
            + nt(tg[2].reshape(256, 256), l_tw[2]))
    for hd in range(8):
        tr_send[hd] = term[32 * hd:32 * hd + 32, :].astype(BF16)

        @pl.when(hd != head)
        def _():
            remote(tr_send.at[hd], tr_recv.at[head], "tr", dev(dy=hd // 2, dc=hd % 2)).start()

        @pl.when(hd == head)
        def _():
            local(tr_send.at[hd], tr_recv.at[head], "tr").start()

    got(b_recv, "bc")
    total = b_own[...] + b_recv[...].astype(F32)
    b_own[...] = total
    for yy in range(4):
        y_send[yy] = total[32 * yy:32 * yy + 32, :].astype(BF16)

        @pl.when(yy != y)
        def _():
            remote(y_send.at[yy], y_recv.at[y], "by", dev(dy=yy)).start()

    got(tr_recv, "tr")
    tback = tr_recv[0].astype(F32)
    for hd in range(1, 8):
        tback = tback + tr_recv[hd].astype(F32)
    cols = pl.ds(pl.multiple_of(x * 768, 768), 768)
    tdn_all[x] = ((1.0 + l_tmod[1:2, cols]) * tback).astype(BF16)
    tnf = l_tnrm[:, cols].astype(F32)
    ts_buf[head] = jnp.concatenate([jnp.sum(tback, axis=0, keepdims=True),
                                    jnp.sum(tback * tnf, axis=0, keepdims=True)], axis=0)
    for xx in range(4):
        @pl.when(xx != x)
        def _():
            remote(tdn_all.at[x], tdn_all.at[x], "tdn", dev(dx=xx)).start()
    for hd in range(8):
        @pl.when(hd != head)
        def _():
            remote(ts_buf.at[head], ts_buf.at[head], "ts", dev(dy=hd // 2, dc=hd % 2)).start()
    got(ts_buf.at[pl.ds(0, 7)], "ts")
    tstat = ts_buf[0]
    for hd in range(1, 8):
        tstat = tstat + ts_buf[hd]
    tsx_buf[x] = tstat
    for xx in range(4):
        @pl.when(xx != x)
        def _():
            remote(tsx_buf.at[x], tsx_buf.at[x], "tsx", dev(dx=xx)).start()

    got(y_recv.at[pl.ds(0, 3)], "by")
    back = b_own[rows32(y), :]
    for yy in range(4):
        back = back + jnp.where(yy == y, 0.0, y_recv[yy].astype(F32))
    o_dn[...] = ((1.0 + l_mod[1:2, :]) * back).astype(BF16)
    stat = jnp.concatenate([jnp.sum(back, axis=0, keepdims=True),
                            jnp.sum(back * l_nrm[...].astype(F32), axis=0, keepdims=True)], axis=0)
    s1_s[0] = stat[:, 0:1536]
    s1_s[1] = stat[:, 1536:3072]
    remote(s1_s.at[1 - c], s1_r, "s1", dev(dc=1 - c)).start()
    got(s1_r, "s1")
    s2_buf[me] = s1_s[c] + s1_r[...]

    def send_s2(t, carry):
        @pl.when(t != me)
        def _():
            remote(s2_buf.at[me], s2_buf.at[me], "s2", dev(dx=t % 4, dy=t // 4)).start()
        return carry

    lax.fori_loop(0, 16, send_s2, 0)
    got(s2_buf.at[pl.ds(0, 15)], "s2")
    stat = s2_buf[0]
    for t in range(1, 16):
        stat = stat + s2_buf[t]
    s3_buf[z] = stat
    for zz in range(4):
        @pl.when(zz != z)
        def _():
            remote(s3_buf.at[z], s3_buf.at[z], "s3", dev(dz=zz)).start()
    got(s3_buf.at[pl.ds(0, 3)], "s3")
    s4_buf[c] = s3_buf[0] + s3_buf[1] + s3_buf[2] + s3_buf[3]
    remote(s4_buf.at[c], s4_buf.at[c], "s4", dev(dc=1 - c)).start()
    got(s4_buf.at[0], "s4")
    o_vs[:, 0:1536] = s4_buf[0]
    o_vs[:, 1536:3072] = s4_buf[1]

    got(tdn_all.at[pl.ds(0, 3)], "tdn")
    got(tsx_buf.at[pl.ds(0, 3)], "tsx")
    for xx in range(4):
        o_tdn[:, 768 * xx:768 * xx + 768] = tdn_all[xx]
        o_ts[:, 768 * xx:768 * xx + 768] = tsx_buf[xx]
    got(tw_r, "tw")
    o_twg[...] += tw_r[...].astype(F32)

    for ch in (1, 2, 0):
        got(w_recv.at[pl.ds(0, 7), 0], "w%d" % ch)
        total = w_own[ch]
        for other in range(8):
            total = total + jnp.where(pos == other, 0.0, w_recv[other, ch].astype(F32))
        o_wg[ch] = total

    for name in ("a_k", "a_v", "a_q", "a_d"):
        sent(kv.at[0, 0, pl.ds(0, 480)], name)

    @pl.when(y == z)
    def _():
        for name in ("a_tk", "a_tv", "a_tq", "a_td"):
            sent(kv.at[0, 0, pl.ds(0, 96)], name)
    sent(d_recv.at[pl.ds(0, 15)], "a_st")

    @pl.when(c == mine)
    def _():
        sent(l_recv.at[pl.ds(0, 3)], "a_lse")
        for ch in range(3):
            sent(kv.at[:, 0, pl.ds(0, 512)], "e%d" % ch)
            sent(kv.at[0, 0, pl.ds(0, 512)], "e%d" % ch)
        for _ in range(3):
            sent(tz, "te")

    @pl.when(c != mine)
    def _():
        sent(l_recv, "a_lse")
        for ch in range(3):
            sent(gr.at[ch], "e%d" % ch)
        for _ in range(4):
            sent(tz, "te")
    sent(kv.at[0], "b_kv")
    for name in ("b_qz", "b_qc", "b_qf"):
        sent(qd.at[0], name)
    for name in ("b_sz", "b_sc", "b_sf"):
        sent(st.at[0], name)
    sent(vin_all.at[pl.ds(0, 31 * 32)], "vin")
    sent(tin_all.at[pl.ds(0, 7 * 32)], "tin")
    sent(dkv_s, "d_kv")
    sent(dqc_s, "d_qc")
    sent(dqz_s, "d_qz")
    sent(tz.at[:, pl.ds(0, 3)], "tz")
    for ch in range(3):
        sent(w_recv.at[pl.ds(0, 7), 0], "w%d" % ch)
    sent(b_send, "bc")
    sent(y_send.at[pl.ds(0, 3)], "by")
    sent(tr_recv.at[pl.ds(0, 7)], "tr")
    sent(tdn_all.at[pl.ds(0, 3)], "tdn")
    sent(ts_buf.at[pl.ds(0, 7)], "ts")
    sent(tsx_buf.at[pl.ds(0, 3)], "tsx")
    sent(s1_r, "s1")
    sent(s2_buf.at[pl.ds(0, 15)], "s2")
    sent(s3_buf.at[pl.ds(0, 3)], "s3")
    sent(s4_buf.at[0], "s4")
    sent(tw_s, "tw")


SCRATCH = (
    ((32, 2048), BF16), ((32, 2048), BF16), ((32, 2048), BF16), ((32, 2048), BF16),
    ((32, D), BF16), ((32, D), BF16), ((3, D, 256), BF16), ((3, 768, 256), BF16),
    ((2, 256), F32), ((2, 256), F32), ((2, D), F32), ((2, D), F32),
    ((4, 2, ROWS, 128), BF16), ((2, 2, ROWS, 128), BF16), ((4, 16, 128), F32),
    ((16, 8, 128), F32), ((16, 8, 128), F32), ((2, 2, 8, 128), F32), ((4, 8, 128), F32),
    ((2, ROWS, 128), F32), ((2, ROWS, 128), F32), ((4, ROWS, 128), F32),
    ((2, ROWS, 128), BF16), ((2, ROWS, 128), BF16), ((2, ROWS, 128), BF16), ((2, ROWS, 128), BF16),
    ((ROWS, 128), BF16), ((ROWS, 128), BF16), ((3, ROWS, 128), BF16),
    ((4, 32, 768), BF16), ((1024, 768), BF16), ((32, D), BF16), ((256, 512), BF16),
    ((3, 1024, 256), BF16), ((3, 4, 32, 128), BF16), ((3, 4, 2, 32, 256), BF16), ((3, 256, 256), BF16),
    ((8, 3, 96, 256), BF16), ((8, 3, 96, 256), BF16), ((3, 96, 256), F32),
    ((128, D), BF16), ((128, D), BF16), ((128, D), F32), ((4, 32, D), BF16), ((4, 32, D), BF16),
    ((512, 256), BF16), ((8, 32, 768), BF16), ((8, 32, 768), BF16), ((4, 32, 768), BF16), ((8, 2, 768), F32), ((4, 2, 768), F32),
    ((2, 2, 1536), F32), ((2, 1536), F32), ((16, 2, 1536), F32), ((4, 2, 1536), F32), ((2, 2, 1536), F32),
    ((3, 96, 256), BF16), ((3, 96, 256), BF16),
)


def body(
    video_q, video_k, video_v, video_out, video_dout, text_q, text_k, text_v, text_out, text_dout,
    video_lse, text_lse, video_norm, text_norm, video_mod, text_mod, video_weight, text_weight,
):
    args = [a[0] for a in (
        video_q, video_k, video_v, video_out, video_dout, text_q, text_k, text_v, text_out, text_dout,
        video_lse, text_lse, video_norm, text_norm, video_mod, text_mod)]
    args += [jnp.transpose(w, (1, 0, 2)) for w in (video_weight, text_weight)]
    vmem = pl.BlockSpec(memory_space=pltpu.VMEM)
    dn, tdn, wg, twg, vs, ts = pl.pallas_call(
        kernel,
        out_shape=(
            jax.ShapeDtypeStruct((32, D), BF16), jax.ShapeDtypeStruct((32, D), BF16),
            jax.ShapeDtypeStruct((3, 96, 256), F32), jax.ShapeDtypeStruct((3, 96, 256), F32),
            jax.ShapeDtypeStruct((2, D), F32), jax.ShapeDtypeStruct((2, D), F32),
        ),
        in_specs=[pl.BlockSpec(memory_space=pl.ANY)] * len(args),
        out_specs=(vmem,) * 6,
        scratch_shapes=[pltpu.VMEM(shape, kind) for shape, kind in SCRATCH] + [
            pltpu.SemaphoreType.DMA((len(NAMES),)),
            pltpu.SemaphoreType.DMA((len(NAMES),)),
            pltpu.SemaphoreType.DMA((len(LOCALS),)),
        ],
        compiler_params=pltpu.CompilerParams(has_side_effects=True, vmem_limit_bytes=60 * 1024 * 1024),
    )(*args)
    return (
        dn[None], tdn[None], jnp.transpose(wg, (1, 0, 2)), jnp.transpose(twg, (1, 0, 2)), vs[None], ts[None],
    )


def solution(mesh):
    tokens = P("dp", ("blk", "head"), None)
    text = P("dp", "head", None)
    whole = P("dp", None, None)
    columns = P(None, None, "head")
    return jax.shard_map(
        body,
        mesh=mesh,
        in_specs=(tokens,) * 5 + (text,) * 5 + (
            P("dp", "head", "blk"), P("dp", "head", None), tokens, text, whole, whole, columns, columns),
        out_specs=(
            tokens, text, P(("dp", "blk"), None, "head"), P(("dp", "blk"), None, "head"), whole, whole),
        check_vma=False,
    )
```

time: 1300 us -> 117 us (0.09)
  blocking collectives: 724 us -> 0 us
  waiting for transfers between devices: 447 us -> 0 us
  Pallas kernels: 0 us -> 107 us
  starting transfers between devices: 36.6 us -> 0 us
  matrix products: 34.2 us -> 0 us
  local copies, waits for them, and re-layouts: 25.3 us -> 9.31 us
  between operations: 16 us -> 0.65 us
  other arithmetic: 13.4 us -> 0 us
    psum x2 -> x0, blocking collectives: 689 us -> none  [the longest x1 665 us: body(): video_total = lax.psum(video_stat, ('blk', 'head'))]
    reduce_scatter x6 -> x0, waiting for transfers between devices: 224 us -> none  [the longest x1 85.8 us: body(): lax.psum_scatter(key_buf.astype(jnp.bfloat16), 'blk', scatter_dimension=0...]
    psum x1 -> x0, waiting for transfers between devices: 126 us -> none  [body(): lax.psum(text_q_part.astype(jnp.bfloat16), 'blk').astype(jnp.float32)]
    pallas_call x0 -> x1, Pallas kernels: none -> 107 us  [body(): pl.pallas_call(kernel, out_shape=(jax.ShapeDtypeStruct((32, D), BF16), ja...]
    all_gather x3 -> x0, waiting for transfers between devices: 60.8 us -> none  [the longest x1 60.8 us: body(): lax.all_gather(head_v, 'blk', axis=0, tiled=True)]
    all_to_all x9 -> x0, starting transfers between devices: 36 us -> none  [the longest x1 4.14 us: body(): lax.all_to_all(text_out[0], 'head', split_axis=1, concat_axis=0, tiled=True)]
    all_to_all x9 -> x0, waiting for transfers between devices: 34.4 us -> none  [the longest x1 5.69 us: body(): lax.all_to_all(text_dout[0], 'head', split_axis=1, concat_axis=0, tiled=T...]
    dot_general x44 -> x0, matrix products: 34.2 us -> none  [the longest x16 10.5 us: dot_rows(): lax.dot_general(left, right, (((1,), (1,)), ((), ())), preferred_element_...]
  transfers between devices with their start and end apart: 19 -> 0, of which waited for: 16 -> 0; matrix products, arithmetic and copies ran while one was open for 5% -> 0% of each run, Pallas kernels for 0% -> 0%
where the time goes in v1:
time: 117 us
  Pallas kernels  107 us (91%)
  local copies, waits for them, and re-layouts  9.31 us (8%)
    pallas_call x1, Pallas kernels, body(): pl.pallas_call(kernel, out_shape=(jax.ShapeDtypeStruct((32, D), BF16), ja...  107 us
    unnamed x6, local copies, waits for them, and re-layouts  9.31 us

profile of v1, /device:TPU:1, one launch (start us, length us, event | category | flops | bytes accessed | tf_op | source)
XLA Modules:
  0.0 117.0 jit_solution(10948416259913834915)
XLA Ops:
  0.6 107.1 %shard_map.217 = (bf16[32,3072]{1,0:T(8,128)(2,1)}, bf16[32,3072]{1,0:T(8,128)(2,1)}, f32[3,96,256]{2,1,0:T(8,128)}, f32[3,96,256]{2,1,0:T(8,128)}, f32[2,3072]{1,0:T(2,128)}, /*index=5*/f32[2,3072]{1,0:T(2,128)}) custom-call(bf16[32,2048]{1,0:T(8,128)(2,1)} %bitcast.32, bf16[32,2048]{1,0:T(8,128)(2,1)} %bitcast.33, bf16[32,2048]{1,0:T(8,128)(2,1)} %bitcast.34, ...), custom_call_target="tpu_custom_call" | custom-call | tf_op jit(solution)/shard_map/pallas_call | solution.py:625
  107.7 1.6 %copy.30 = bf16[1,32,3072]{2,1,0:T(8,128)(2,1)} copy(bf16[1,32,3072]{2,1,0:T(8,128)(2,1)} %bitcast.29) | data formatting | bytes 393216
  109.3 1.6 %copy.31 = bf16[1,32,3072]{2,1,0:T(8,128)(2,1)} copy(bf16[1,32,3072]{2,1,0:T(8,128)(2,1)} %bitcast.28) | data formatting | bytes 393216
  110.9 1.7 %copy.32 = f32[96,3,256]{2,0,1:T(8,128)} copy(f32[96,3,256]{2,0,1:T(8,128)} %bitcast.27) | data formatting | bytes 589824
  112.6 1.7 %copy.33 = f32[96,3,256]{2,0,1:T(8,128)} copy(f32[96,3,256]{2,0,1:T(8,128)} %bitcast.26) | data formatting | bytes 589824
  114.3 1.3 %copy.34 = f32[1,2,3072]{2,1,0:T(2,128)} copy(f32[1,2,3072]{2,1,0:T(2,128)} %bitcast.45) | data formatting | bytes 49152
  115.7 1.3 %copy.35 = f32[1,2,3072]{2,1,0:T(2,128)} copy(f32[1,2,3072]{2,1,0:T(2,128)} %bitcast.44) | data formatting | bytes 49152

commit v2 on v1

--- a/solution.py
+++ b/solution.py
@@ -20,9 +20,9 @@
 
 NAMES = (
     "a_q", "a_d", "a_k", "a_v", "a_st", "a_lse", "a_tq", "a_td", "a_tk", "a_tv",
-    "b_kv", "b_qc", "b_sc", "b_qz", "b_sz", "b_qf", "b_sf", "vin", "tin",
+    "b_kv", "b_qc", "b_sc", "b_qz", "b_sz", "b_qf", "b_sf", "vin", "vf", "tin",
     "d_kv", "d_qc", "d_qz", "e0", "e1", "e2", "tz", "te", "w0", "w1", "w2",
-    "bc", "by", "tr", "tdn", "ts", "tsx", "s1", "s2", "s3", "s4", "tw",
+    "bc0", "bc1", "bc2", "bc3", "bc4", "bc5", "by", "tr", "tdn", "ts", "tsx", "s1", "s2", "s3", "tw",
 )
 SEM = {name: index for index, name in enumerate(NAMES)}
 LOCALS = ("out", "dout", "tout", "tdout", "nrm", "tnrm", "w", "tw", "lse", "tlse", "mod", "tmod")
@@ -40,15 +40,22 @@
     return jnp.dot(left, right, preferred_element_type=F32)
 
 
-def kernel(
+def kernel(*refs):
+    drains = []
+    kernel_body(drains, *refs)
+    drains[0]()
+
+
+def kernel_body(
+    drains,
     q, k, v, out, dout, tq, tk, tv, tout, tdout, lse, tlse, norm, tnorm, mod, tmod, weight, tweight,
     o_dn, o_tdn, o_wg, o_twg, o_vs, o_ts,
     l_out, l_dout, l_tout, l_tdout, l_nrm, l_tnrm, l_w, l_tw, l_lse, l_tlse, l_mod, l_tmod,
     qd, kv, st, d_send, d_recv, l_send, l_recv,
     gk_acc, gv_acc, gq_acc, dkv_s, dkv_r, dqc_s, dqc_r, dqz_s, dqz_r, g_fin,
-    vin_s, vin_all, tin_s, tin_all, gr, tz, tg, gs,
+    vin_s, vin_all, p_mod, gain_col, shift_col, m_acc, s_acc, tin_s, tin_all, gr, tz, tg, gs,
     w_send, w_recv, w_own, b_send, b_recv, b_own, y_send, y_recv,
-    t_tmp, tr_send, tr_recv, tdn_all, ts_buf, tsx_buf, s1_s, s1_r, s2_buf, s3_buf, s4_buf, tw_s, tw_r,
+    t_tmp, tr_send, tr_recv, tdn_all, ts_buf, tsx_buf, s1_buf, s2_buf, s3_buf, tw_s, tw_r,
     rs, ss, ls,
 ):
     dp = lax.axis_index("dp")
@@ -76,49 +83,122 @@
 
     def got(ref, name):
         pltpu.make_async_copy(ref, ref, rs.at[SEM[name]]).wait()
+        if name in expected:
+            expected[name].pop(0)
 
     def sent(ref, name):
         pltpu.make_async_copy(ref, ref, ss.at[SEM[name]]).wait()
 
+    expected = {}
+    copies = {}
+    leaving = []
+
+    def expect(name, *refs):
+        expected[name] = list(refs)
+
+    def drain():
+        for name, refs in list(expected.items()):
+            for ref in list(refs):
+                got(ref, name)
+        for n_, cp in list(copies.items()):
+            if n_ not in waited:
+                cp.wait()
+        for fn in leaving:
+            fn()
+
+    waited = set()
+    drains.append(drain)
+
+    def ready(name):
+        copies[name].wait()
+        waited.add(name)
+
+    def leave(ref, name, times=1):
+        def fn():
+            for _ in range(times):
+                sent(ref, name)
+        leaving.append(fn)
+
+    def leave_if(cond, ref, name, times=1):
+        def fn():
+            @pl.when(cond)
+            def _():
+                for _ in range(times):
+                    sent(ref, name)
+        leaving.append(fn)
+
     def rows32(index):
         return pl.ds(pl.multiple_of(index * 32, 32), 32)
 
     def lanes(index, width=128):
         return pl.ds(pl.multiple_of(index * width, 128), width)
 
-    def send_a(t, carry):
-        to = dev(dx=t % 4, dy=t // 4)
-        for src, dst, name in ((k, kv.at[0, 0], "a_k"), (v, kv.at[0, 1], "a_v"),
-                               (q, qd.at[0, 0], "a_q"), (dout, qd.at[0, 1], "a_d")):
-            piece = src.at[:, lanes(t)]
-            place = dst.at[rows32(me)]
-
-            @pl.when(t != me)
-            def _():
-                remote(piece, place, name, to).start()
-
-            @pl.when(t == me)
-            def _():
-                local(piece, place, name).start()
+    barrier = pltpu.get_barrier_semaphore()
+
+    def greet(t, carry):
+        hd, xx = t // 4, t % 4
+
+        @pl.when(jnp.logical_or(hd != head, xx != x))
+        def _():
+            pl.semaphore_signal(barrier, inc=1, device_id=dev(dx=xx, dy=hd // 2, dc=hd % 2), device_id_type=MESH)
         return carry
 
-    lax.fori_loop(0, 16, send_a, 0)
-
-    @pl.when(y == z)
-    def _():
-        for t in range(4):
-            for src, dst, name in ((tk, kv.at[0, 0], "a_tk"), (tv, kv.at[0, 1], "a_tv"),
-                                   (tq, qd.at[0, 0], "a_tq"), (tdout, qd.at[0, 1], "a_td")):
-                piece = src.at[:, lanes(4 * t + x)]
-                place = dst.at[pl.ds(SET, TXT)]
-
-                @pl.when(t != y)
+    def greet_line(t, carry):
+        @pl.when(t != dp * 4 + z)
+        def _():
+            pl.semaphore_signal(barrier, inc=1, device_id=dev(ddp=t // 4, dz=t % 4), device_id_type=MESH)
+        return carry
+
+    lax.fori_loop(0, 32, greet, 0)
+    lax.fori_loop(0, 8, greet_line, 0)
+    pl.semaphore_wait(barrier, 38)
+
+    def send_a(table):
+        def step(t, carry):
+            to = dev(dx=t % 4, dy=t // 4)
+            for src, dst, name in table:
+                piece = src.at[:, lanes(t)]
+                place = dst.at[rows32(me)]
+
+                @pl.when(t != me)
                 def _():
-                    remote(piece, place, name, dev(dy=t)).start()
-
-                @pl.when(t == y)
+                    remote(piece, place, name, to).start()
+
+                @pl.when(t == me)
                 def _():
                     local(piece, place, name).start()
+            return carry
+
+        lax.fori_loop(0, 16, step, 0)
+
+    def send_text(table):
+        @pl.when(y == z)
+        def _():
+            for t in range(4):
+                for src, dst, name in table:
+                    piece = src.at[:, lanes(4 * t + x)]
+                    place = dst.at[pl.ds(SET, TXT)]
+
+                    @pl.when(t != y)
+                    def _():
+                        remote(piece, place, name, dev(dy=t)).start()
+
+                    @pl.when(t == y)
+                    def _():
+                        local(piece, place, name).start()
+
+    send_a(((k, kv.at[0, 0], "a_k"), (v, kv.at[0, 1], "a_v")))
+    send_text(((tk, kv.at[0, 0], "a_tk"), (tv, kv.at[0, 1], "a_tv")))
+    send_a(((q, qd.at[0, 0], "a_q"), (dout, qd.at[0, 1], "a_d")))
+    send_text(((tq, qd.at[0, 0], "a_tq"), (tdout, qd.at[0, 1], "a_td")))
+    for name, ref in (("a_k", kv.at[0, 0, pl.ds(0, SET)]), ("a_v", kv.at[0, 1, pl.ds(0, SET)]),
+                      ("a_q", qd.at[0, 0, pl.ds(0, SET)]), ("a_d", qd.at[0, 1, pl.ds(0, SET)])):
+        expect(name, ref)
+        leave(kv.at[0, 0, pl.ds(0, 480)], name)
+    for name, ref in (("a_tk", kv.at[0, 0, pl.ds(SET, TXT)]), ("a_tv", kv.at[0, 1, pl.ds(SET, TXT)]),
+                      ("a_tq", qd.at[0, 0, pl.ds(SET, TXT)]), ("a_td", qd.at[0, 1, pl.ds(SET, TXT)])):
+        expect(name, ref)
+        leave_if(y == z, kv.at[0, 0, pl.ds(0, 96)], name)
 
     loads = {
         "out": (out, l_out), "dout": (dout, l_dout), "tout": (tout, l_tout), "tdout": (tdout, l_tdout),
@@ -126,9 +206,10 @@
         "mod": (mod, l_mod), "tmod": (tmod, l_tmod), "w": (weight, l_w),
         "tw": (tweight.at[:, pl.ds(pl.multiple_of(x * 768, 768), 768), :], l_tw),
     }
-    copies = {n: pltpu.make_async_copy(s, d, ls.at[LOCALS.index(n)]) for n, (s, d) in loads.items()}
+    copies.update({n: pltpu.make_async_copy(s, d, ls.at[LOCALS.index(n)]) for n, (s, d) in loads.items()})
     for name in ("out", "dout", "lse", "tlse", "tout", "tdout", "nrm", "mod", "tnrm", "tmod", "w", "tw"):
         copies[name].start()
+
 
     lane = lax.broadcasted_iota(jnp.int32, (16, 128), 1)
     ones = jnp.where(
@@ -144,11 +225,11 @@
             total = total + nt(ones, jnp.concatenate([part] * 4, axis=0))
         return total
 
-    copies["out"].wait()
-    copies["dout"].wait()
+    ready("out")
+    ready("dout")
     video_delta = jnp.where(lane // 32 == x, delta_rows(l_out, l_dout), 0.0)
-    copies["tout"].wait()
-    copies["tdout"].wait()
+    ready("tout")
+    ready("tdout")
     text_delta = jnp.where(lane < 32, delta_rows(l_tout, l_tdout), 0.0)
     d_send[...] = jnp.zeros_like(d_send)
     for h in range(16):
@@ -166,9 +247,11 @@
         return carry
 
     lax.fori_loop(0, 16, send_delta, 0)
-
-    copies["lse"].wait()
-    copies["tlse"].wait()
+    expect("a_st", d_recv)
+    leave(d_recv.at[pl.ds(0, 15)], "a_st")
+
+    ready("lse")
+    ready("tlse")
     lane8 = lax.broadcasted_iota(jnp.int32, (8, 128), 1)
     l_send[...] = jnp.zeros_like(l_send)
     for j in range(2):
@@ -194,15 +277,22 @@
             def _():
                 local(l_send.at[j, cc], l_recv.at[x], "a_lse").start()
 
-    copies["nrm"].wait()
-    copies["mod"].wait()
-    gain = 1.0 + l_mod[1:2, :]
-    vin = (gain * l_nrm[...].astype(F32) + l_mod[0:1, :])
+    expect("a_lse", l_recv)
+    leave_if(c == mine, l_recv.at[pl.ds(0, 3)], "a_lse")
+    leave_if(c != mine, l_recv, "a_lse")
+
+    ready("nrm")
+    ready("mod")
+
+    def group(value, xx):
+        return jnp.concatenate([value[:, 384 * m + 96 * xx:384 * m + 96 * xx + 96] for m in range(8)], axis=1)
+
+    nrm = l_nrm[...].astype(F32)
     for xx in range(4):
-        parts = [vin[:, 384 * m + 96 * xx:384 * m + 96 * xx + 96] for m in range(8)]
-        vin_s[xx] = jnp.concatenate(parts, axis=1).astype(BF16)
-    copies["tnrm"].wait()
-    copies["tmod"].wait()
+        vin_s[xx] = group(nrm, xx).astype(BF16)
+        p_mod[xx, 0:2, :] = group(l_mod[...], xx)
+    ready("tnrm")
+    ready("tmod")
     tgain = 1.0 + l_tmod[1:2, :]
     tin_s[...] = (tgain * l_tnrm[...].astype(F32) + l_tmod[0:1, :]).astype(BF16)
 
@@ -217,12 +307,18 @@
     zn = z + 1 - 2 * (z % 2)
     zf = (z + 2) % 4
     remote(kv.at[0], kv.at[1], "b_kv", dev(dz=zn)).start()
+    expect("b_kv", kv.at[1])
+    leave(kv.at[0], "b_kv")
     got(qd.at[0, 0, pl.ds(0, SET)], "a_q")
     got(qd.at[0, 1, pl.ds(0, SET)], "a_d")
     got(qd.at[0, 0, pl.ds(SET, TXT)], "a_tq")
     got(qd.at[0, 1, pl.ds(SET, TXT)], "a_td")
     remote(qd.at[0], qd.at[1], "b_qz", dev(dz=zf)).start()
     remote(qd.at[0], qd.at[2], "b_qc", dev(dc=1 - c)).start()
+    expect("b_qc", qd.at[2])
+    expect("b_qz", qd.at[1])
+    leave(qd.at[0], "b_qc")
+    leave(qd.at[0], "b_qz")
     got(d_recv, "a_st")
     got(l_recv, "a_lse")
     for yy in range(4):
@@ -235,22 +331,27 @@
     st[0, 10:16, :] = jnp.zeros((6, 128), F32)
     remote(st.at[0], st.at[1], "b_sz", dev(dz=zf)).start()
     remote(st.at[0], st.at[2], "b_sc", dev(dc=1 - c)).start()
+    expect("b_sc", st.at[2])
+    expect("b_sz", st.at[1])
+    leave(st.at[0], "b_sc")
+    leave(st.at[0], "b_sz")
 
     def send_vin(t, carry):
-        hd, xx = t // 4, t % 4
         place = vin_all.at[pl.ds(pl.multiple_of(c * SET + me * 32, 32), 32)]
-        own = jnp.logical_and(hd == head, xx == x)
-
-        @pl.when(jnp.logical_not(own))
-        def _():
-            remote(vin_s.at[xx], place, "vin", dev(dx=xx, dy=hd // 2, dc=hd % 2)).start()
-
-        @pl.when(own)
-        def _():
-            local(vin_s.at[xx], place, "vin").start()
+
+        @pl.when(t != me)
+        def _():
+            remote(vin_s.at[t % 4], place, "vin", dev(dx=t % 4, dy=t // 4)).start()
+
+        @pl.when(t == me)
+        def _():
+            local(vin_s.at[t % 4], place, "vin").start()
         return carry
 
-    lax.fori_loop(0, 32, send_vin, 0)
+    lax.fori_loop(0, 16, send_vin, 0)
+    own_rows = pl.ds(pl.multiple_of(c * SET, SET), SET)
+    expect("vin", vin_all.at[own_rows])
+    leave(vin_all.at[pl.ds(0, 15 * 32)], "vin")
 
     window = jnp.minimum((blk * 96) // 128 * 128, 1280)
 
@@ -269,6 +370,8 @@
         return carry
 
     lax.fori_loop(0, 8, send_tin, 0)
+    expect("tin", tin_all)
+    leave(tin_all.at[pl.ds(0, 7 * 32)], "tin")
 
     def pair(lse_row, delta_row, query, dquery, keys, values):
         probs = jnp.exp2(nt(keys, query) * (FACTOR * LOG2E) - lse_row)
@@ -329,18 +432,30 @@
             gq_acc[i, SET:ROWS, :] += from_text[32 * i:32 * i + 32, :]
 
     lax.fori_loop(0, 6, attend, 0)
+    leave(qd.at[0], "b_qf")
+    leave(st.at[0], "b_sf")
     attend_text(1)
     dkv_s[0] = (gk_acc[1] * FACTOR).astype(BF16)
     dkv_s[1] = gv_acc[1].astype(BF16)
     remote(dkv_s, dkv_r, "d_kv", dev(dz=zn)).start()
+    expect("d_kv", dkv_r)
+    leave(dkv_s, "d_kv")
+    got(vin_all.at[own_rows], "vin")
+    remote(vin_all.at[own_rows], vin_all.at[own_rows], "vf", dev(dc=1 - c)).start()
+    expect("vf", vin_all.at[own_rows])
+    leave(vin_all.at[own_rows], "vf")
     lax.fori_loop(6, 8, attend, 0)
     attend_text(0)
     dqc_s[0] = (gq_acc[2] * FACTOR).astype(BF16)
     dqc_s[1] = (gq_acc[3] * FACTOR).astype(BF16)
     remote(dqc_s, dqc_r, "d_qc", dev(dc=1 - c)).start()
+    expect("d_qc", dqc_r)
+    leave(dqc_s, "d_qc")
     got(dqc_r, "d_qc")
     dqz_s[...] = (gq_acc[1] * FACTOR + dqc_r[1].astype(F32)).astype(BF16)
     remote(dqz_s, dqz_r, "d_qz", dev(dz=zf)).start()
+    expect("d_qz", dqz_r)
+    leave(dqz_s, "d_qz")
 
     def send_grads(ch):
         for xx in range(4):
@@ -364,6 +479,12 @@
     got(dqz_r, "d_qz")
     g_fin[0] = (gq_acc[0] * FACTOR + dqc_r[0].astype(F32) + dqz_r[...].astype(F32)).astype(BF16)
     send_grads(0)
+    for ch in range(3):
+        name = "e%d" % ch
+        expect(name, gr.at[ch])
+        leave_if(c == mine, kv.at[:, 0, pl.ds(0, SET)], name)
+        leave_if(c == mine, kv.at[0, 0, pl.ds(0, SET)], name)
+        leave_if(c != mine, gr.at[ch], name)
 
     for zz in range(4):
         piece = g_fin.at[:, pl.ds(SET, TXT)]
@@ -376,6 +497,7 @@
         def _():
             local(piece, tz.at[:, z], "tz").start()
     got(tz, "tz")
+    leave(tz.at[:, pl.ds(0, 3)], "tz")
     for xx in range(4):
         own = jnp.logical_and(x == xx, c == mine)
         place = tg.at[:, :, c, :, lanes(half)]
@@ -388,16 +510,26 @@
         def _():
             local(tz, place, "te").start()
 
+    expect("te", tg)
+    leave_if(c == mine, tz, "te", 3)
+    leave_if(c != mine, tz, "te", 4)
+
     pos = dp * 4 + z
-    got(vin_all, "vin")
-    for ch in (1, 2, 0):
-        got(gr.at[ch], "e%d" % ch)
+    wide = jnp.ones((8, 1024), BF16)
+
+    def project(ch):
+        if ch:
+            got(gr.at[ch], "e%d" % ch)
         grads = gr[ch]
+        m_acc[...] = tn(vin_all[...], grads)
+        col = nn(wide, grads)[0:1, :]
         for other in range(8):
-            if other % 4 == 0:
-                term = tn(vin_all[:, 96 * other:96 * other + 384], grads)
-            piece = term[96 * (other % 4):96 * (other % 4) + 96, :]
-            w_send[other, ch] = piece.astype(BF16)
+            rows = slice(96 * other, 96 * other + 96)
+            part = m_acc[rows, :]
+            gain = jnp.concatenate([gain_col[rows, :]] * 2, axis=1)
+            shift = jnp.concatenate([shift_col[rows, :]] * 2, axis=1)
+            term = gain * part + shift * col
+            w_send[other, ch] = term.astype(BF16)
 
             @pl.when(pos != other)
             def _():
@@ -406,14 +538,46 @@
 
             @pl.when(pos == other)
             def _():
-                w_own[ch] = piece
+                w_own[ch] = term
+        expect("w%d" % ch, w_recv.at[pl.ds(0, 7), ch])
+        leave(w_recv.at[pl.ds(0, 7), ch], "w%d" % ch)
+        for other in range(8):
+            rows = slice(96 * other, 96 * other + 96)
+            first = pl.multiple_of((other // 4) * 1536 + (other % 4) * 384 + x * 96, 32)
+            wq = l_w[ch, pl.ds(first, 96), :].astype(F32)
+            zero, one = wq * col, wq * m_acc[rows, :]
+            s_acc[0, rows, :] += zero[:, 0:128] + zero[:, 128:256]
+            s_acc[1, rows, :] += one[:, 0:128] + one[:, 128:256]
+
+    quarter = jnp.broadcast_to(p_mod[x, 0:1, :], (128, 768))
+    shift_col[...] = jnp.transpose(quarter)
+    quarter = jnp.broadcast_to(1.0 + p_mod[x, 1:2, :], (128, 768))
+    gain_col[...] = jnp.transpose(quarter)
+    s_acc[...] = jnp.zeros_like(s_acc)
+    ready("w")
+    got(vin_all.at[own_rows], "vf")
+    project(1)
+    project(2)
+
+    got(gr.at[0], "e0")
 
     for ch in range(3):
         for cc in range(2):
             for yy in range(4):
                 first = pl.multiple_of(cc * SET + (yy * 4 + x) * 32, 32)
                 gs[ch, cc * 128 + yy * 32:cc * 128 + yy * 32 + 32, :] = gr[ch, pl.ds(first, 32), :]
-    copies["w"].wait()
+    def gather_chunk(n):
+        cols = slice(512 * n, 512 * n + 512)
+        got(b_recv.at[:, cols], "bc%d" % n)
+        total = b_own[:, cols] + b_recv[:, cols].astype(F32)
+        b_own[:, cols] = total
+        for yy in range(4):
+            y_send[yy, :, cols] = total[32 * yy:32 * yy + 32, :].astype(BF16)
+
+            @pl.when(yy != y)
+            def _():
+                remote(y_send.at[yy, :, cols], y_recv.at[y, :, cols], "by", dev(dy=yy)).start()
+
     for n in range(6):
         cols = slice(512 * n, 512 * n + 512)
         term = (nt(gs[0], l_w[0, cols, :]) + nt(gs[1], l_w[1, cols, :]) + nt(gs[2], l_w[2, cols, :]))
@@ -427,7 +591,22 @@
         def _():
             b_own[:, cols] = term[128:256, :]
             b_send[:, cols] = term[0:128, :].astype(BF16)
-    remote(b_send, b_recv, "bc", dev(dc=1 - c)).start()
+        remote(b_send.at[:, cols], b_recv.at[:, cols], "bc%d" % n, dev(dc=1 - c)).start()
+        leave(b_send.at[:, cols], "bc%d" % n)
+        if n:
+            gather_chunk(n - 1)
+    gather_chunk(5)
+    expect("by", y_recv.at[pl.ds(0, 3)])
+    leave(y_send.at[pl.ds(0, 3)], "by")
+    project(0)
+    for n in range(2):
+        s1_buf[head, n:n + 1, :] = jnp.sum(jnp.transpose(s_acc[n]), axis=0, keepdims=True)
+    for hd in range(8):
+        @pl.when(hd != head)
+        def _():
+            remote(s1_buf.at[head], s1_buf.at[head], "s1", dev(dy=hd // 2, dc=hd % 2)).start()
+    expect("s1", s1_buf.at[pl.ds(0, 7)])
+    leave(s1_buf.at[pl.ds(0, 7)], "s1")
 
     got(tg, "te")
     got(tin_all, "tin")
@@ -441,7 +620,9 @@
         tw_s[ch] = t_tmp[pl.ds(away, 96), :]
         o_twg[ch] = t_tmp[pl.ds(near, 96), :].astype(F32)
     remote(tw_s, tw_r, "tw", dev(ddp=1 - dp)).start()
-    copies["tw"].wait()
+    expect("tw", tw_r)
+    leave(tw_s, "tw")
+    ready("tw")
     term = (nt(tg[0].reshape(256, 256), l_tw[0]) + nt(tg[1].reshape(256, 256), l_tw[1])
             + nt(tg[2].reshape(256, 256), l_tw[2]))
     for hd in range(8):
@@ -455,15 +636,20 @@
         def _():
             local(tr_send.at[hd], tr_recv.at[head], "tr").start()
 
-    got(b_recv, "bc")
-    total = b_own[...] + b_recv[...].astype(F32)
-    b_own[...] = total
-    for yy in range(4):
-        y_send[yy] = total[32 * yy:32 * yy + 32, :].astype(BF16)
-
-        @pl.when(yy != y)
-        def _():
-            remote(y_send.at[yy], y_recv.at[y], "by", dev(dy=yy)).start()
+    expect("tr", tr_recv)
+    leave(tr_recv.at[pl.ds(0, 7)], "tr")
+
+    got(s1_buf.at[pl.ds(0, 7)], "s1")
+    stat = s1_buf[0]
+    for hd in range(1, 8):
+        stat = stat + s1_buf[hd]
+    s2_buf[z] = stat
+    for zz in range(4):
+        @pl.when(zz != z)
+        def _():
+            remote(s2_buf.at[z], s2_buf.at[z], "s2", dev(dz=zz)).start()
+    expect("s2", s2_buf.at[pl.ds(0, 3)])
+    leave(s2_buf.at[pl.ds(0, 3)], "s2")
 
     got(tr_recv, "tr")
     tback = tr_recv[0].astype(F32)
@@ -478,10 +664,21 @@
         @pl.when(xx != x)
         def _():
             remote(tdn_all.at[x], tdn_all.at[x], "tdn", dev(dx=xx)).start()
+    expect("tdn", tdn_all.at[pl.ds(0, 3)])
+    leave(tdn_all.at[pl.ds(0, 3)], "tdn")
     for hd in range(8):
         @pl.when(hd != head)
         def _():
             remote(ts_buf.at[head], ts_buf.at[head], "ts", dev(dy=hd // 2, dc=hd % 2)).start()
+    leave(ts_buf.at[pl.ds(0, 7)], "ts")
+    got(s2_buf.at[pl.ds(0, 3)], "s2")
+    s3_buf[x] = s2_buf[0] + s2_buf[1] + s2_buf[2] + s2_buf[3]
+    for xx in range(4):
+        @pl.when(xx != x)
+        def _():
+            remote(s3_buf.at[x], s3_buf.at[x], "s3", dev(dx=xx)).start()
+    expect("s3", s3_buf.at[pl.ds(0, 3)])
+    leave(s3_buf.at[pl.ds(0, 3)], "s3")
     got(ts_buf.at[pl.ds(0, 7)], "ts")
     tstat = ts_buf[0]
     for hd in range(1, 8):
@@ -491,42 +688,19 @@
         @pl.when(xx != x)
         def _():
             remote(tsx_buf.at[x], tsx_buf.at[x], "tsx", dev(dx=xx)).start()
+    expect("tsx", tsx_buf.at[pl.ds(0, 3)])
+    leave(tsx_buf.at[pl.ds(0, 3)], "tsx")
+
 
     got(y_recv.at[pl.ds(0, 3)], "by")
     back = b_own[rows32(y), :]
     for yy in range(4):
         back = back + jnp.where(yy == y, 0.0, y_recv[yy].astype(F32))
     o_dn[...] = ((1.0 + l_mod[1:2, :]) * back).astype(BF16)
-    stat = jnp.concatenate([jnp.sum(back, axis=0, keepdims=True),
-                            jnp.sum(back * l_nrm[...].astype(F32), axis=0, keepdims=True)], axis=0)
-    s1_s[0] = stat[:, 0:1536]
-    s1_s[1] = stat[:, 1536:3072]
-    remote(s1_s.at[1 - c], s1_r, "s1", dev(dc=1 - c)).start()
-    got(s1_r, "s1")
-    s2_buf[me] = s1_s[c] + s1_r[...]
-
-    def send_s2(t, carry):
-        @pl.when(t != me)
-        def _():
-            remote(s2_buf.at[me], s2_buf.at[me], "s2", dev(dx=t % 4, dy=t // 4)).start()
-        return carry
-
-    lax.fori_loop(0, 16, send_s2, 0)
-    got(s2_buf.at[pl.ds(0, 15)], "s2")
-    stat = s2_buf[0]
-    for t in range(1, 16):
-        stat = stat + s2_buf[t]
-    s3_buf[z] = stat
-    for zz in range(4):
-        @pl.when(zz != z)
-        def _():
-            remote(s3_buf.at[z], s3_buf.at[z], "s3", dev(dz=zz)).start()
     got(s3_buf.at[pl.ds(0, 3)], "s3")
-    s4_buf[c] = s3_buf[0] + s3_buf[1] + s3_buf[2] + s3_buf[3]
-    remote(s4_buf.at[c], s4_buf.at[c], "s4", dev(dc=1 - c)).start()
-    got(s4_buf.at[0], "s4")
-    o_vs[:, 0:1536] = s4_buf[0]
-    o_vs[:, 1536:3072] = s4_buf[1]
+    for m in range(8):
+        o_vs[:, 384 * m:384 * m + 384] = jnp.concatenate(
+            [s3_buf[xx, 0:2, 96 * m:96 * m + 96] for xx in range(4)], axis=1)
 
     got(tdn_all.at[pl.ds(0, 3)], "tdn")
     got(tsx_buf.at[pl.ds(0, 3)], "tsx")
@@ -543,55 +717,16 @@
             total = total + jnp.where(pos == other, 0.0, w_recv[other, ch].astype(F32))
         o_wg[ch] = total
 
-    for name in ("a_k", "a_v", "a_q", "a_d"):
-        sent(kv.at[0, 0, pl.ds(0, 480)], name)
-
-    @pl.when(y == z)
-    def _():
-        for name in ("a_tk", "a_tv", "a_tq", "a_td"):
-            sent(kv.at[0, 0, pl.ds(0, 96)], name)
-    sent(d_recv.at[pl.ds(0, 15)], "a_st")
-
-    @pl.when(c == mine)
-    def _():
-        sent(l_recv.at[pl.ds(0, 3)], "a_lse")
-        for ch in range(3):
-            sent(kv.at[:, 0, pl.ds(0, 512)], "e%d" % ch)
-            sent(kv.at[0, 0, pl.ds(0, 512)], "e%d" % ch)
-        for _ in range(3):
-            sent(tz, "te")
-
-    @pl.when(c != mine)
-    def _():
-        sent(l_recv, "a_lse")
-        for ch in range(3):
-            sent(gr.at[ch], "e%d" % ch)
-        for _ in range(4):
-            sent(tz, "te")
-    sent(kv.at[0], "b_kv")
-    for name in ("b_qz", "b_qc", "b_qf"):
-        sent(qd.at[0], name)
-    for name in ("b_sz", "b_sc", "b_sf"):
-        sent(st.at[0], name)
-    sent(vin_all.at[pl.ds(0, 31 * 32)], "vin")
-    sent(tin_all.at[pl.ds(0, 7 * 32)], "tin")
-    sent(dkv_s, "d_kv")
-    sent(dqc_s, "d_qc")
-    sent(dqz_s, "d_qz")
-    sent(tz.at[:, pl.ds(0, 3)], "tz")
-    for ch in range(3):
-        sent(w_recv.at[pl.ds(0, 7), 0], "w%d" % ch)
-    sent(b_send, "bc")
-    sent(y_send.at[pl.ds(0, 3)], "by")
-    sent(tr_recv.at[pl.ds(0, 7)], "tr")
-    sent(tdn_all.at[pl.ds(0, 3)], "tdn")
-    sent(ts_buf.at[pl.ds(0, 7)], "ts")
-    sent(tsx_buf.at[pl.ds(0, 3)], "tsx")
-    sent(s1_r, "s1")
-    sent(s2_buf.at[pl.ds(0, 15)], "s2")
-    sent(s3_buf.at[pl.ds(0, 3)], "s3")
-    sent(s4_buf.at[0], "s4")
-    sent(tw_s, "tw")
+def finish(*refs):
+    into = [pltpu.make_async_copy(refs[n], refs[12 + n], refs[18].at[n]) for n in range(6)]
+    back = [pltpu.make_async_copy(refs[12 + n], refs[6 + n], refs[18].at[n]) for n in range(6)]
+    for copy in into:
+        copy.start()
+    for first, second in zip(into, back):
+        first.wait()
+        second.start()
+    for copy in back:
+        copy.wait()
 
 
 SCRATCH = (
@@ -603,12 +738,13 @@
     ((2, ROWS, 128), F32), ((2, ROWS, 128), F32), ((4, ROWS, 128), F32),
     ((2, ROWS, 128), BF16), ((2, ROWS, 128), BF16), ((2, ROWS, 128), BF16), ((2, ROWS, 128), BF16),
     ((ROWS, 128), BF16), ((ROWS, 128), BF16), ((3, ROWS, 128), BF16),
-    ((4, 32, 768), BF16), ((1024, 768), BF16), ((32, D), BF16), ((256, 512), BF16),
+    ((4, 32, 768), BF16), ((1024, 768), BF16), ((4, 8, 768), F32), ((768, 128), F32), ((768, 128), F32),
+    ((768, 256), F32), ((2, 768, 128), F32), ((32, D), BF16), ((256, 512), BF16),
     ((3, 1024, 256), BF16), ((3, 4, 32, 128), BF16), ((3, 4, 2, 32, 256), BF16), ((3, 256, 256), BF16),
     ((8, 3, 96, 256), BF16), ((8, 3, 96, 256), BF16), ((3, 96, 256), F32),
     ((128, D), BF16), ((128, D), BF16), ((128, D), F32), ((4, 32, D), BF16), ((4, 32, D), BF16),
     ((512, 256), BF16), ((8, 32, 768), BF16), ((8, 32, 768), BF16), ((4, 32, 768), BF16), ((8, 2, 768), F32), ((4, 2, 768), F32),
-    ((2, 2, 1536), F32), ((2, 1536), F32), ((16, 2, 1536), F32), ((4, 2, 1536), F32), ((2, 2, 1536), F32),
+    ((8, 8, 768), F32), ((4, 8, 768), F32), ((4, 8, 768), F32),
     ((3, 96, 256), BF16), ((3, 96, 256), BF16),
 )
 
@@ -622,7 +758,7 @@
         video_lse, text_lse, video_norm, text_norm, video_mod, text_mod)]
     args += [jnp.transpose(w, (1, 0, 2)) for w in (video_weight, text_weight)]
     vmem = pl.BlockSpec(memory_space=pltpu.VMEM)
-    dn, tdn, wg, twg, vs, ts = pl.pallas_call(
+    results = pl.pallas_call(
         kernel,
         out_shape=(
             jax.ShapeDtypeStruct((32, D), BF16), jax.ShapeDtypeStruct((32, D), BF16),
@@ -636,8 +772,17 @@
             pltpu.SemaphoreType.DMA((len(NAMES),)),
             pltpu.SemaphoreType.DMA((len(LOCALS),)),
         ],
-        compiler_params=pltpu.CompilerParams(has_side_effects=True, vmem_limit_bytes=60 * 1024 * 1024),
+        compiler_params=pltpu.CompilerParams(collective_id=0, has_side_effects=True, vmem_limit_bytes=60 * 1024 * 1024),
     )(*args)
+    anywhere = pl.BlockSpec(memory_space=pl.ANY)
+    dn, tdn, wg, twg, vs, ts = pl.pallas_call(
+        finish,
+        out_shape=[jax.ShapeDtypeStruct(r.shape, r.dtype) for r in results],
+        in_specs=[anywhere] * 6,
+        out_specs=[anywhere] * 6,
+        scratch_shapes=[pltpu.VMEM(r.shape, r.dtype) for r in results] + [pltpu.SemaphoreType.DMA((6,))],
+        compiler_params=pltpu.CompilerParams(vmem_limit_bytes=60 * 1024 * 1024),
+    )(*results)
     return (
         dn[None], tdn[None], jnp.transpose(wg, (1, 0, 2)), jnp.transpose(twg, (1, 0, 2)), vs[None], ts[None],
     )

time: 117 us -> 99.3 us (0.85)
  local copies, waits for them, and re-layouts: 9.31 us -> 0 us
  Pallas kernels: 107 us -> 98.5 us
    pallas_call x1, Pallas kernels: 107 us -> 96.5 us  [body(): pl.pallas_call(kernel, out_shape=(jax.ShapeDtypeStruct((32, D), BF16), ja...]
    unnamed x6 -> x0, local copies, waits for them, and re-layouts: 9.31 us -> none
    pallas_call x0 -> x1, Pallas kernels: none -> 2.03 us  [body(): pl.pallas_call(finish, out_shape=[jax.ShapeDtypeStruct(r.shape, r.dtype)...]
where the time goes in v2:
time: 99.3 us; the launch traced here: 99.2 us
  Pallas kernels  98.5 us (99%)
    pallas_call x1, Pallas kernels, body(): pl.pallas_call(kernel, out_shape=(jax.ShapeDtypeStruct((32, D), BF16), ja...  96.5 us
    pallas_call x1, Pallas kernels, body(): pl.pallas_call(finish, out_shape=[jax.ShapeDtypeStruct(r.shape, r.dtype)...  2.03 us

profile of v2, /device:TPU:1, one launch (start us, length us, event | category | flops | bytes accessed | tf_op | source)
XLA Modules:
  0.0 99.2 jit_solution(18257688448947846337)
XLA Ops:
  0.6 96.5 %shard_map.217 = (bf16[32,3072]{1,0:T(8,128)(2,1)}, bf16[32,3072]{1,0:T(8,128)(2,1)}, f32[3,96,256]{2,1,0:T(8,128)}, f32[3,96,256]{2,1,0:T(8,128)}, f32[2,3072]{1,0:T(2,128)}, /*index=5*/f32[2,3072]{1,0:T(2,128)}) custom-call(bf16[32,2048]{1,0:T(8,128)(2,1)} %bitcast.28, bf16[32,2048]{1,0:T(8,128)(2,1)} %bitcast.29, bf16[32,2048]{1,0:T(8,128)(2,1)} %bitcast.30, ...), custom_call_target="tpu_custom_call" | custom-call | tf_op jit(solution)/shard_map/pallas_call | solution.py:761
  97.2 2.0 %shard_map.218 = (bf16[32,3072]{1,0:T(8,128)(2,1)}, bf16[32,3072]{1,0:T(8,128)(2,1)}, f32[3,96,256]{2,1,0:T(8,128)}, f32[3,96,256]{2,1,0:T(8,128)}, f32[2,3072]{1,0:T(2,128)}, /*index=5*/f32[2,3072]{1,0:T(2,128)}) custom-call(bf16[32,3072]{1,0:T(8,128)(2,1)} %get-tuple-element.18.refs_0_, bf16[32,3072]{1,0:T(8,128)(2,1)} %get-tuple-element.19.refs_1_, ...), custom_call_target="tpu_custom_call" | custom-call | tf_op jit(solution)/shard_map/pallas_call | solution.py:778

commit v3 on v2

v3 whole, which is shorter than its diff:
```python
import functools

import jax
import jax.numpy as jnp
from jax import lax
from jax.experimental import pallas as pl
from jax.experimental.pallas import tpu as pltpu
from jax.sharding import PartitionSpec as P

MESH = pl.DeviceIdType.MESH
D = 3072
DH = 128
SET = 512
ROWS = 544
TXT = 32
FACTOR = DH ** (-0.5)
LOG2E = 1.4426950408889634
F32 = jnp.float32
BF16 = jnp.bfloat16

NAMES = (
    "a_q", "a_d", "a_k", "a_v", "a_st", "a_lse", "a_tq", "a_td", "a_tk", "a_tv",
    "b_kv", "b_qc", "b_sc", "b_qz", "b_sz", "b_qf", "b_sf", "v0", "wq", "tin", "tq",
    "d_kv", "d_qc", "d_qz", "gkv", "gq", "e", "tz", "te",
    "bc0", "bc1", "bc2", "bc3", "bc4", "bc5", "by", "tr", "tdn", "ts", "tsx", "s1", "s2", "s3", "tw", "fin",
)
RING = tuple("r%d%d%d" % (way, step, ch) for way in range(2) for step in range(4) for ch in range(3))
INPUTS = tuple("v1%d%d" % (t, n) for t in (1, 2, 3) for n in range(4)) + tuple("v2%d" % n for n in range(4))
NAMES = NAMES + RING + INPUTS
SEM = {name: index for index, name in enumerate(NAMES)}
LOCALS = ("out", "dout", "tout", "tdout", "nrm", "tnrm", "w", "tw", "lse", "tlse", "mod", "tmod")


def nt(left, right):
    return lax.dot_general(left, right, (((1,), (1,)), ((), ())), preferred_element_type=F32)


def tn(left, right):
    return lax.dot_general(left, right, (((0,), (0,)), ((), ())), preferred_element_type=F32)


def nn(left, right):
    return jnp.dot(left, right, preferred_element_type=F32)


def kernel(*refs):
    drains = []
    kernel_body(drains, *refs)
    drains[0]()


def kernel_body(
    drains,
    q, k, v, out, dout, tq, tk, tv, tout, tdout, lse, tlse, norm, tnorm, mod, tmod, weight, tweight,
    r_dn, r_tdn, r_wg, r_twg, r_vs, r_ts,
    o_dn, o_tdn, o_wg, o_twg, o_vs, o_ts,
    l_out, l_dout, l_tout, l_tdout, l_nrm, l_tnrm, l_w, l_tw, l_lse, l_tlse, l_mod, l_tmod,
    qd, kv, st, d_send, d_recv, l_send, l_recv,
    gk_acc, gv_acc, gq_acc, dkv_s, dkv_r, dqc_s, dqc_r, dqz_s, dqz_r, gw, g_txt,
    vin_s, vin_all, wq, gain_col, shift_col, m_acc, s_acc, tin_s, tin_all, tq_all, tz, tg, gs,
    wt, ring_s, ring_r, fin_s, fin_r, b_send, b_recv, b_own, y_send, y_recv,
    t_tmp, tr_send, tr_recv, tdn_all, ts_buf, tsx_buf, s1_buf, s2_buf, s3_buf, tw_s, tw_r,
    rs, ss, ls, os_,
):
    results = (r_dn, r_tdn, r_wg, r_twg, r_vs, r_ts)
    dp = lax.axis_index("dp")
    blk = lax.axis_index("blk")
    head = lax.axis_index("head")
    z, x, y, c = blk // 4, blk % 4, head // 2, head % 2
    me = y * 4 + x
    mine = x // 2
    half = x % 2

    def dev(dz=None, dx=None, dy=None, dc=None, ddp=None):
        zz = z if dz is None else dz
        xx = x if dx is None else dx
        yy = y if dy is None else dy
        cc = c if dc is None else dc
        return {"dp": dp if ddp is None else ddp, "blk": zz * 4 + xx, "head": yy * 2 + cc}

    def remote(src, dst, name, to):
        return pltpu.make_async_remote_copy(
            src_ref=src, dst_ref=dst, send_sem=ss.at[SEM[name]], recv_sem=rs.at[SEM[name]],
            device_id=to, device_id_type=MESH)

    def local(src, dst, name):
        return pltpu.make_async_copy(src, dst, rs.at[SEM[name]])

    def got(ref, name):
        pltpu.make_async_copy(ref, ref, rs.at[SEM[name]]).wait()
        if name in expected:
            expected[name].pop(0)

    def sent(ref, name):
        pltpu.make_async_copy(ref, ref, ss.at[SEM[name]]).wait()

    expected = {}
    copies = {}
    leaving = []

    def expect(name, *refs):
        expected[name] = list(refs)

    def drain():
        for name, refs in list(expected.items()):
            for ref in list(refs):
                got(ref, name)
        for n_, cp in list(copies.items()):
            if n_ not in waited:
                cp.wait()
        for fn in leaving:
            fn()

    waited = set()
    drains.append(drain)

    def ready(name):
        copies[name].wait()
        waited.add(name)

    def leave(ref, name, times=1):
        def fn():
            for _ in range(times):
                sent(ref, name)
        leaving.append(fn)

    def leave_if(cond, ref, name, times=1):
        def fn():
            @pl.when(cond)
            def _():
                for _ in range(times):
                    sent(ref, name)
        leaving.append(fn)

    def rows32(index):
        return pl.ds(pl.multiple_of(index * 32, 32), 32)

    def lanes(index, width=128):
        return pl.ds(pl.multiple_of(index * width, 128), width)

    barrier = pltpu.get_barrier_semaphore()

    plane = [(i, j) for i in (2, 1, 3, 0) for j in (2, 1, 3, 0) if (i, j) != (0, 0)]
    pos = dp * 4 + z

    def chip(i, j):
        return (x + i) % 4, (y + j) % 4

    def along_z(t):
        at = (pos + t) % 8
        return dev(ddp=at // 4, dz=at % 4)

    greeted = [dev(dx=chip(i, j)[0], dy=chip(i, j)[1]) for i, j in plane]
    greeted += [along_z(t) for t in (4, 3, 5, 2, 6, 1, 7)]
    greeted += [dev(dx=(x + i) % 4, dc=1 - c) for i in (2, 1, 3)]
    greeted += [dev(dy=(y + j) % 4, dc=1 - c) for j in (2, 1, 3)] + [dev(dc=1 - c)]
    for to in greeted:
        pl.semaphore_signal(barrier, inc=1, device_id=to, device_id_type=MESH)
    pl.semaphore_wait(barrier, 29)

    def send_a(table):
        place_at = rows32(me)
        for i, j in plane + [(0, 0)]:
            xx, yy = chip(i, j)
            to = dev(dx=xx, dy=yy)
            for src, dst, name in table:
                piece = src.at[:, lanes(4 * yy + xx)]
                if (i, j) == (0, 0):
                    local(piece, dst.at[place_at], name).start()
                else:
                    remote(piece, dst.at[place_at], name, to).start()

    def send_text(table):
        @pl.when(y == z)
        def _():
            for j in (2, 1, 3, 0):
                yy = (y + j) % 4
                for src, dst, name in table:
                    piece = src.at[:, lanes(4 * yy + x)]
                    place = dst.at[pl.ds(SET, TXT)]
                    if j:
                        remote(piece, place, name, dev(dy=yy)).start()
                    else:
                        local(piece, place, name).start()

    send_a(((k, kv.at[0, 0], "a_k"), (v, kv.at[0, 1], "a_v")))
    send_text(((tk, kv.at[0, 0], "a_tk"), (tv, kv.at[0, 1], "a_tv")))
    send_a(((q, qd.at[0, 0], "a_q"), (dout, qd.at[0, 1], "a_d")))
    send_text(((tq, qd.at[0, 0], "a_tq"), (tdout, qd.at[0, 1], "a_td")))
    for name, ref in (("a_k", kv.at[0, 0, pl.ds(0, SET)]), ("a_v", kv.at[0, 1, pl.ds(0, SET)]),
                      ("a_q", qd.at[0, 0, pl.ds(0, SET)]), ("a_d", qd.at[0, 1, pl.ds(0, SET)])):
        expect(name, ref)
        leave(kv.at[0, 0, pl.ds(0, 480)], name)
    for name, ref in (("a_tk", kv.at[0, 0, pl.ds(SET, TXT)]), ("a_tv", kv.at[0, 1, pl.ds(SET, TXT)]),
                      ("a_tq", qd.at[0, 0, pl.ds(SET, TXT)]), ("a_td", qd.at[0, 1, pl.ds(SET, TXT)])):
        expect(name, ref)
        leave_if(y == z, kv.at[0, 0, pl.ds(0, 96)], name)

    @pl.when(c == mine)
    def _():
        for core in range(2):
            for m in range(8):
                piece = weight.at[:, pl.ds(384 * m + 192 * core, 192), lanes(half)]
                place = wq.at[:, pl.ds(192 * m, 192), :]

                @pl.when(c != core)
                def _():
                    remote(piece, place, "wq", dev(dc=core)).start()

                @pl.when(c == core)
                def _():
                    local(piece, place, "wq").start()
    expect("wq", wq)
    leave_if(c == mine, wq, "wq")
    loads = {
        "out": (out, l_out), "dout": (dout, l_dout), "tout": (tout, l_tout), "tdout": (tdout, l_tdout),
        "nrm": (norm, l_nrm), "tnrm": (tnorm, l_tnrm), "lse": (lse, l_lse), "tlse": (tlse, l_tlse),
        "mod": (mod, l_mod), "tmod": (tmod, l_tmod), "w": (weight, l_w),
        "tw": (tweight.at[:, pl.ds(pl.multiple_of(x * 768, 768), 768), :], l_tw),
    }
    copies.update({n: pltpu.make_async_copy(s, d, ls.at[LOCALS.index(n)]) for n, (s, d) in loads.items()})
    for name in ("out", "dout", "lse", "tlse", "tout", "tdout", "nrm", "mod", "tnrm", "tmod", "w", "tw"):
        copies[name].start()


    lane = lax.broadcasted_iota(jnp.int32, (16, 128), 1)
    ones = jnp.where(
        lax.broadcasted_iota(jnp.int32, (16, 2048), 1) // DH
        == lax.broadcasted_iota(jnp.int32, (16, 2048), 0), 1.0, 0.0).astype(BF16)

    def delta_rows(a_ref, b_ref):
        total = jnp.zeros((16, 128), F32)
        products = a_ref[...].astype(F32) * b_ref[...].astype(F32)
        high = products.astype(BF16)
        low = (products - high.astype(F32)).astype(BF16)
        for part in (high, low):
            total = total + nt(ones, jnp.concatenate([part] * 4, axis=0))
        return total

    ready("out")
    ready("dout")
    video_delta = jnp.where(lane // 32 == x, delta_rows(l_out, l_dout), 0.0)
    ready("tout")
    ready("tdout")
    text_delta = jnp.where(lane < 32, delta_rows(l_tout, l_tdout), 0.0)
    d_send[...] = jnp.zeros_like(d_send)
    for h in range(16):
        d_send[h, 0:1, :] = video_delta[h:h + 1, :]
        d_send[h, 1:2, :] = text_delta[h:h + 1, :]

    for i, j in plane:
        xx, yy = chip(i, j)
        remote(d_send.at[yy * 4 + xx], d_recv.at[me], "a_st", dev(dx=xx, dy=yy)).start()
    local(d_send.at[me], d_recv.at[me], "a_st").start()
    expect("a_st", d_recv)
    leave(d_recv.at[pl.ds(0, 15)], "a_st")

    ready("lse")
    ready("tlse")
    lane8 = lax.broadcasted_iota(jnp.int32, (8, 128), 1)
    l_send[...] = jnp.zeros_like(l_send)
    for j in range(2):
        for cc in range(2):
            for yy in range(4):
                row = jnp.broadcast_to(l_lse[j:j + 1, 128 * (yy // 2):128 * (yy // 2) + 128], (8, 128))
                shift = (32 * x + 256 - (yy % 2) * 64 - cc * 32) % 128
                row = jnp.where(lane8 // 32 == x, pltpu.roll(row, shift, 1), 0.0)
                l_send[j, cc, yy:yy + 1, :] = row[0:1, :]
            row = jnp.broadcast_to(l_tlse[j:j + 1, pl.ds(pl.multiple_of((z // 2) * 128, 128), 128)], (8, 128))
            shift = (256 - (z % 2) * 64 - cc * 32) % 128
            row = jnp.where(lane8 < 32, pltpu.roll(row, shift, 1), 0.0)
            l_send[j, cc, 4:5, :] = row[0:1, :]
    for j in range(2):
        for cc in range(2):
            own = jnp.logical_and(x == 2 * c + j, c == cc)

            @pl.when(jnp.logical_not(own))
            def _():
                remote(l_send.at[j, cc], l_recv.at[x], "a_lse", dev(dx=2 * c + j, dc=cc)).start()

            @pl.when(own)
            def _():
                local(l_send.at[j, cc], l_recv.at[x], "a_lse").start()

    expect("a_lse", l_recv)
    leave_if(c == mine, l_recv.at[pl.ds(0, 3)], "a_lse")
    leave_if(c != mine, l_recv, "a_lse")

    ready("nrm")
    ready("mod")

    def group(value, core):
        return jnp.concatenate([value[:, 384 * m + 192 * core:384 * m + 192 * core + 192] for m in range(8)], axis=1)

    nrm = l_nrm[...].astype(F32)
    for core in range(2):
        vin_s[core] = group(nrm, core).astype(BF16)
    local(vin_s.at[c], vin_all.at[c, y, x], "v0").start()
    remote(vin_s.at[1 - c], vin_all.at[c, y, x], "v0", dev(dc=1 - c)).start()
    expect("v0", vin_all.at[:, y, x])
    leave(vin_s.at[0], "v0")
    grouped = jnp.where(c == 0, group(l_mod[...], 0), group(l_mod[...], 1))
    shift_col[...] = jnp.transpose(jnp.broadcast_to(grouped[0:1, :], (128, 1536)))
    gain_col[...] = jnp.transpose(jnp.broadcast_to(1.0 + grouped[1:2, :], (128, 1536)))
    ready("tnrm")
    ready("tmod")
    tgain = 1.0 + l_tmod[1:2, :]
    tin_s[...] = (tgain * l_tnrm[...].astype(F32) + l_tmod[0:1, :]).astype(BF16)

    along = jnp.where(c == 0, y, x)

    def line_one(t):
        to = (along + t) % 4
        return dev(dx=jnp.where(c == 0, x, to), dy=jnp.where(c == 0, to, y))

    def line_two(t):
        to = (jnp.where(c == 0, x, y) + t) % 4
        return dev(dx=jnp.where(c == 0, to, x), dy=jnp.where(c == 0, y, to))

    first_pair = ((pos + 4) // 2) % 4
    pairs = [(first_pair + n) % 4 for n in (0, 1, 3, 2)]
    chunk = [pl.ds(pl.multiple_of(384 * i, 128), 384) for i in pairs]

    def block(t, n):
        at = (along + 4 - t) % 4
        return vin_all.at[:, jnp.where(c == 0, at, y), jnp.where(c == 0, x, at), :, chunk[n]]

    got(vin_all.at[:, y, x], "v0")
    for n in range(4):
        for t in (2, 1, 3):
            name = "v1%d%d" % (t, n)
            remote(block(0, n), block(0, n), name, line_one(t)).start()
            expect(name, block(t, n))
            leave(block(0, n), name)
        for t in (2, 1, 3):
            remote(block(0, n), block(0, n), "v2%d" % n, line_two(t)).start()
    gk_acc[...] = jnp.zeros_like(gk_acc)
    gv_acc[...] = jnp.zeros_like(gv_acc)
    gq_acc[...] = jnp.zeros_like(gq_acc)

    zn = z + 1 - 2 * (z % 2)
    zf = (z + 2) % 4

    got(kv.at[0, 0, pl.ds(0, SET)], "a_k")
    got(kv.at[0, 1, pl.ds(0, SET)], "a_v")
    got(kv.at[0, 0, pl.ds(SET, TXT)], "a_tk")
    got(kv.at[0, 1, pl.ds(SET, TXT)], "a_tv")

    def pass_on(src, dst, name, to):
        remote(src, dst, name, to).start()
        expect(name, dst)
        leave(src, name)

    pass_on(kv.at[0], kv.at[1], "b_kv", dev(dz=zn))
    got(qd.at[0, 0, pl.ds(0, SET)], "a_q")
    got(qd.at[0, 1, pl.ds(0, SET)], "a_d")
    got(qd.at[0, 0, pl.ds(SET, TXT)], "a_tq")
    got(qd.at[0, 1, pl.ds(SET, TXT)], "a_td")
    pass_on(qd.at[0], qd.at[1], "b_qz", dev(dz=zf))
    pass_on(qd.at[0], qd.at[2], "b_qc", dev(dc=1 - c))
    got(d_recv, "a_st")
    got(l_recv, "a_lse")
    for yy in range(4):
        st[0, yy:yy + 1, :] = LOG2E * (l_recv[0, yy:yy + 1, :] + l_recv[1, yy:yy + 1, :]
                                       + l_recv[2, yy:yy + 1, :] + l_recv[3, yy:yy + 1, :])
        st[0, 4 + yy:5 + yy, :] = (d_recv[4 * yy, 0:1, :] + d_recv[4 * yy + 1, 0:1, :]
                                   + d_recv[4 * yy + 2, 0:1, :] + d_recv[4 * yy + 3, 0:1, :])
    st[0, 8:9, :] = LOG2E * l_recv[0, 4:5, :]
    st[0, 9:10, :] = d_recv[z * 4 + x, 1:2, :]
    st[0, 10:16, :] = jnp.zeros((6, 128), F32)
    remote(st.at[0], st.at[1], "b_sz", dev(dz=zf)).start()
    remote(st.at[0], st.at[2], "b_sc", dev(dc=1 - c)).start()
    expect("b_sc", st.at[2])
    expect("b_sz", st.at[1])
    leave(st.at[0], "b_sc")
    leave(st.at[0], "b_sz")

    def forward(n):
        for t in (1, 3, 2):
            got(block(t, n), "v1%d%d" % (t, n))
            for u in (2, 1, 3):
                remote(block(t, n), block(t, n), "v2%d" % n, line_two(u)).start()

    for n in range(4):
        every = vin_all.at[:, pl.ds(0, 3), :, :, chunk[n]]
        expect("v2%d" % n, every)
        leave(every, "v2%d" % n)

    window = jnp.minimum((blk * 96) // 128 * 128, 1280)

    peers = [(j, m) for j in (2, 1, 3, 0) for m in (0, 1) if (j, m) != (0, 0)]
    quarter = pl.ds(pl.multiple_of(x * 768, 768), 768)

    def to_peers(copies_for, name):
        for j, m in peers:
            yy, cc = (y + j) % 4, (c + m) % 2
            for src, dst in copies_for(yy * 2 + cc):
                remote(src, dst, name, dev(dy=yy, dc=cc)).start()

    def tin_copies(hd):
        return [(tin_s.at[:, pl.ds(pl.multiple_of(other * 1536 + window, 128), 256)],
                 tin_all.at[rows32(head), pl.ds(other * 256, 256)]) for other in range(2)]

    for src, dst in tin_copies(head):
        local(src, dst, "tin").start()
    to_peers(tin_copies, "tin")
    place = tq_all.at[rows32(head)]
    local(l_tnrm.at[:, quarter], place, "tq").start()
    to_peers(lambda hd: [(l_tnrm.at[:, quarter], place)], "tq")
    expect("tq", tq_all)
    leave(tq_all.at[pl.ds(0, 7 * 32)], "tq")
    expect("tin", tin_all)
    leave(tin_all.at[pl.ds(0, 7 * 32)], "tin")

    def pair(lse_row, delta_row, query, dquery, keys, values):
        probs = jnp.exp2(nt(keys, query) * (FACTOR * LOG2E) - lse_row)
        dscores = (probs * (nt(values, dquery) - delta_row)).astype(BF16)
        return probs.astype(BF16), dscores

    def row512(i, first):
        return jnp.concatenate([st[i, first + n:first + n + 1, :] for n in range(4)], axis=1)

    def attend(step, carry):
        i = (step % 2) * 2 + step // 4
        j = ((step + 2) // 4) % 2

        @pl.when(step == 1)
        def _():
            got(qd.at[2], "b_qc")
            got(st.at[2], "b_sc")

        @pl.when(step == 2)
        def _():
            forward(0)
            forward(1)
            got(kv.at[1], "b_kv")

        @pl.when(step == 3)
        def _():
            forward(2)
            forward(3)

        @pl.when(step == 4)
        def _():
            got(qd.at[1], "b_qz")
            remote(qd.at[1], qd.at[3], "b_qf", dev(dc=1 - c)).start()
            got(st.at[1], "b_sz")
            remote(st.at[1], st.at[3], "b_sf", dev(dc=1 - c)).start()

        @pl.when(step == 5)
        def _():
            got(qd.at[3], "b_qf")
            got(st.at[3], "b_sf")

        query, dquery = qd[i, 0, 0:SET, :], qd[i, 1, 0:SET, :]
        keys, values = kv[j, 0], kv[j, 1]
        probs, dscores = pair(row512(i, 0), row512(i, 4), query, dquery, keys, values)
        gv_acc[j] += nn(probs, dquery)
        gk_acc[j] += nn(dscores, query)
        gq_acc[i, 0:SET, :] += tn(dscores, keys)
        return carry

    def attend_text(j):
        query = jnp.concatenate([qd[i, 0, SET:ROWS, :] for i in range(4)], axis=0)
        dquery = jnp.concatenate([qd[i, 1, SET:ROWS, :] for i in range(4)], axis=0)
        lse_row = jnp.zeros((8, 128), F32)
        delta_row = jnp.zeros((8, 128), F32)
        for i in range(4):
            one, two = (jnp.broadcast_to(st[i, r:r + 1, :], (8, 128)) for r in (8, 9))
            lse_row = lse_row + (pltpu.roll(one, 32 * i, 1) if i else one)
            delta_row = delta_row + (pltpu.roll(two, 32 * i, 1) if i else two)
        keys, values = kv[j, 0], kv[j, 1]
        probs, dscores = pair(lse_row[0:1, :], delta_row[0:1, :], query, dquery, keys, values)
        gv_acc[j] += nn(probs, dquery)
        gk_acc[j] += nn(dscores, query)
        from_text = tn(dscores, keys)
        for i in range(4):
            gq_acc[i, SET:ROWS, :] += from_text[32 * i:32 * i + 32, :]

    lax.fori_loop(0, 6, attend, 0)
    leave(qd.at[0], "b_qf")
    leave(st.at[0], "b_sf")
    attend_text(1)
    dkv_s[0] = (gk_acc[1] * FACTOR).astype(BF16)
    dkv_s[1] = gv_acc[1].astype(BF16)
    remote(dkv_s, dkv_r, "d_kv", dev(dz=zn)).start()
    expect("d_kv", dkv_r)
    leave(dkv_s, "d_kv")
    lax.fori_loop(6, 8, attend, 0)
    attend_text(0)
    dqc_s[0] = (gq_acc[2] * FACTOR).astype(BF16)
    dqc_s[1] = (gq_acc[3] * FACTOR).astype(BF16)
    remote(dqc_s, dqc_r, "d_qc", dev(dc=1 - c)).start()
    expect("d_qc", dqc_r)
    leave(dqc_s, "d_qc")
    got(dqc_r, "d_qc")
    dqz_s[...] = (gq_acc[1] * FACTOR + dqc_r[1].astype(F32)).astype(BF16)
    remote(dqz_s, dqz_r, "d_qz", dev(dz=zf)).start()
    expect("d_qz", dqz_r)
    leave(dqz_s, "d_qz")

    def send_grads(name, cols, table):
        own_part = gw.at[c, :, :, :, cols]
        remote(own_part, own_part, name, dev(dc=1 - c)).start()
        expect(name, gw.at[1 - c, :, :, :, cols])
        leave(own_part, name)
        for ch in table:
            for xx in (2, 1, 3, 0):
                to = (x + xx) % 4
                own = jnp.logical_and(xx == 0, c == mine)
                piece = gw.at[c, :, to, :, pl.ds(128 * ch, 128)]
                place = gs.at[c, :, :, pl.ds(pl.multiple_of(256 * ch + 128 * half, 128), 128)]

                @pl.when(jnp.logical_not(own))
                def _():
                    remote(piece, place, "e", dev(dx=to, dc=mine)).start()

                @pl.when(own)
                def _():
                    local(piece, place, "e").start()

    def finish_channel(ch, value):
        gw[c, :, :, :, 128 * ch:128 * ch + 128] = value[0:SET, :].reshape(4, 4, 32, 128)
        g_txt[ch] = value[SET:ROWS, :]

    got(dkv_r, "d_kv")
    finish_channel(1, (gk_acc[0] * FACTOR + dkv_r[0].astype(F32)).astype(BF16))
    finish_channel(2, (gv_acc[0] + dkv_r[1].astype(F32)).astype(BF16))
    send_grads("gkv", pl.ds(128, 256), (1, 2))
    got(dqz_r, "d_qz")
    finish_channel(0, (gq_acc[0] * FACTOR + dqc_r[0].astype(F32) + dqz_r[...].astype(F32)).astype(BF16))
    send_grads("gq", pl.ds(0, 128), (0,))
    expect("e", gs)
    for ch in range(3):
        one = gw.at[0, :, 0, :, pl.ds(128 * ch, 128)]
        leave_if(c == mine, one, "e", 3)
        leave_if(c != mine, one, "e", 4)
    for zz in range(4):
        @pl.when(z != zz)
        def _():
            remote(g_txt, tz.at[:, z], "tz", dev(dz=zz)).start()

        @pl.when(z == zz)
        def _():
            local(g_txt, tz.at[:, z], "tz").start()
    expect("tz", tz)
    leave(tz.at[:, pl.ds(0, 3)], "tz")

    got(gw.at[1 - c, :, :, :, pl.ds(128, 256)], "gkv")
    got(gw.at[1 - c, :, :, :, pl.ds(0, 128)], "gq")
    grads = gw[...].reshape(1024, 384)
    col = nn(jnp.ones((8, 1024), BF16), grads)[0:1, :]

    def project(n):
        i = pairs[n]
        got(vin_all.at[:, pl.ds(0, 3), :, :, chunk[n]], "v2%d" % n)
        cols = pl.ds(pl.multiple_of(384 * i, 128), 384)
        part = tn(vin_all[:, :, :, :, cols].reshape(1024, 384), grads)
        m_acc[cols, :] = part
        gain = jnp.concatenate([gain_col[cols, :]] * 3, axis=1)
        shift = jnp.concatenate([shift_col[cols, :]] * 3, axis=1)
        term = gain * part + shift * col
        wt[2 * i] = term[0:192, :]
        wt[2 * i + 1] = term[192:384, :]

    def ring_to(way):
        to = (pos + (1 if way == 0 else 7)) % 8
        return dev(ddp=to // 4, dz=to % 4)

    def ring(step):
        for ch in range(3):
            lane_cols = slice(128 * ch, 128 * ch + 128)
            for way in range(2):
                dest = (pos + (4 - step if way == 0 else 4 + step)) % 8
                rows = (slice(0, 96) if way == 0 else slice(96, 192)) if step == 0 else slice(0, 192)
                own = wt[dest, rows, lane_cols]
                if step:
                    size = 96 if step == 1 else 192
                    heard = ring_r.at[way, step - 1, ch, pl.ds(0, size)]
                    got(heard, "r%d%d%d" % (way, step - 1, ch))
                    heard = heard[...].astype(F32)
                    if step == 1:
                        near, far = own[0:96, :], own[96:192, :]
                        pair_ = (near + heard, far) if way == 0 else (near, far + heard)
                        own = jnp.concatenate(pair_, axis=0)
                    else:
                        own = own + heard
                size = 96 if step == 0 else 192
                out_ref = ring_s.at[way, step, ch, pl.ds(0, size)]
                out_ref[...] = own.astype(BF16)
                name = "r%d%d%d" % (way, step, ch)
                remote(out_ref, ring_r.at[way, step, ch, pl.ds(0, size)], name, ring_to(way)).start()
                expect(name, ring_r.at[way, step, ch, pl.ds(0, size)])
                leave(out_ref, name)

    project(0)
    ring(0)
    got(tz, "tz")
    for xx in (2, 1, 3, 0):
        to = (x + xx) % 4
        own = jnp.logical_and(xx == 0, c == mine)
        place = tg.at[:, :, c, :, lanes(half)]

        @pl.when(jnp.logical_not(own))
        def _():
            remote(tz, place, "te", dev(dx=to, dc=mine)).start()

        @pl.when(own)
        def _():
            local(tz, place, "te").start()
    expect("te", tg)
    leave_if(c == mine, tz, "te", 3)
    leave_if(c != mine, tz, "te", 4)
    project(1)
    project(2)
    project(3)
    got(wq, "wq")
    for m in range(8):
        rows = slice(192 * m, 192 * m + 192)
        zero = jnp.zeros((192, 128), F32)
        one = jnp.zeros((192, 128), F32)
        for ch in range(3):
            w_part = wq[ch, rows, :].astype(F32)
            zero = zero + w_part * col[:, 128 * ch:128 * ch + 128]
            one = one + w_part * m_acc[rows, 128 * ch:128 * ch + 128]
        s_acc[0, rows, :] = zero
        s_acc[1, rows, :] = one
    for n in range(2):
        high = s_acc[n].astype(BF16)
        low = (s_acc[n] - high.astype(F32)).astype(BF16)
        row = jnp.ones((8, 128), BF16)
        s1_buf[me, n:n + 1, :] = (nt(row, high) + nt(row, low))[0:1, :]

    for i, j in plane:
        remote(s1_buf.at[me], s1_buf.at[me], "s1", dev(dx=chip(i, j)[0], dy=chip(i, j)[1])).start()
    expect("s1", s1_buf.at[pl.ds(0, 15)])
    leave(s1_buf.at[pl.ds(0, 15)], "s1")
    ring(1)

    def back_chunk(n):
        cols = slice(512 * n, 512 * n + 512)
        rows = gs[...].reshape(256, 768)
        term = (nt(rows[:, 0:256], l_w[0, cols, :]) + nt(rows[:, 256:512], l_w[1, cols, :])
                + nt(rows[:, 512:768], l_w[2, cols, :]))

        @pl.when(c == 0)
        def _():
            b_own[:, cols] = term[0:128, :]
            b_send[:, cols] = term[128:256, :].astype(BF16)

        @pl.when(c == 1)
        def _():
            b_own[:, cols] = term[128:256, :]
            b_send[:, cols] = term[0:128, :].astype(BF16)
        remote(b_send.at[:, cols], b_recv.at[:, cols], "bc%d" % n, dev(dc=1 - c)).start()
        expect("bc%d" % n, b_recv.at[:, cols])
        leave(b_send.at[:, cols], "bc%d" % n)

    def gather_chunk(n):
        cols = slice(512 * n, 512 * n + 512)
        got(b_recv.at[:, cols], "bc%d" % n)
        total = b_own[:, cols] + b_recv[:, cols].astype(F32)
        b_own[:, cols] = total
        for yy in range(4):
            y_send[yy, :, cols] = total[32 * yy:32 * yy + 32, :].astype(BF16)

            @pl.when(yy != y)
            def _():
                remote(y_send.at[yy, :, cols], y_recv.at[y, :, cols], "by", dev(dy=yy)).start()

    ready("w")
    got(gs, "e")
    back_chunk(0)
    back_chunk(1)
    gather_chunk(0)
    back_chunk(2)
    gather_chunk(1)
    back_chunk(3)
    gather_chunk(2)
    back_chunk(4)
    gather_chunk(3)
    back_chunk(5)
    gather_chunk(4)
    gather_chunk(5)
    expect("by", y_recv.at[pl.ds(0, 3)])
    leave(y_send.at[pl.ds(0, 3)], "by")
    ring(2)

    got(tg, "te")
    ready("tw")
    term = (nt(tg[0].reshape(256, 256), l_tw[0]) + nt(tg[1].reshape(256, 256), l_tw[1])
            + nt(tg[2].reshape(256, 256), l_tw[2]))
    for hd in range(8):
        tr_send[hd] = term[32 * hd:32 * hd + 32, :].astype(BF16)
    local(tr_send.at[head], tr_recv.at[head], "tr").start()
    to_peers(lambda hd: [(tr_send.at[hd], tr_recv.at[head])], "tr")
    expect("tr", tr_recv)
    leave(tr_recv.at[pl.ds(0, 7)], "tr")
    got(tq_all, "tq")
    ts_buf[head] = jnp.concatenate([jnp.sum(term, axis=0, keepdims=True),
                                    jnp.sum(term * tq_all[...].astype(F32), axis=0, keepdims=True)], axis=0)
    to_peers(lambda hd: [(ts_buf.at[head], ts_buf.at[head])], "ts")
    expect("ts", ts_buf.at[pl.ds(0, 7)])
    leave(ts_buf.at[pl.ds(0, 7)], "ts")

    got(tin_all, "tin")
    first = pl.multiple_of(blk * 96 - window, 32)
    away = pl.multiple_of((1 - dp) * 256 + first, 32)
    near = pl.multiple_of(dp * 256 + first, 32)
    for ch in range(3):
        t_tmp[...] = tn(tin_all[...], tg[ch].reshape(256, 256)).astype(BF16)
        tw_s[ch] = t_tmp[pl.ds(away, 96), :]
        o_twg[ch] = t_tmp[pl.ds(near, 96), :].astype(F32)
    remote(tw_s, tw_r, "tw", dev(ddp=1 - dp)).start()
    expect("tw", tw_r)
    leave(tw_s, "tw")

    got(s1_buf.at[pl.ds(0, 15)], "s1")
    stat = s1_buf[0]
    for t in range(1, 16):
        stat = stat + s1_buf[t]
    s2_buf[z] = stat
    for t in (2, 1, 3):
        remote(s2_buf.at[z], s2_buf.at[z], "s2", dev(dz=(z + t) % 4)).start()
    expect("s2", s2_buf.at[pl.ds(0, 3)])
    leave(s2_buf.at[pl.ds(0, 3)], "s2")
    ring(3)
    got(ts_buf.at[pl.ds(0, 7)], "ts")
    tstat = ts_buf[0]
    for hd in range(1, 8):
        tstat = tstat + ts_buf[hd]
    tsx_buf[x] = tstat
    for t in (2, 1, 3):
        remote(tsx_buf.at[x], tsx_buf.at[x], "tsx", dev(dx=(x + t) % 4)).start()
    expect("tsx", tsx_buf.at[pl.ds(0, 3)])
    leave(tsx_buf.at[pl.ds(0, 3)], "tsx")
    got(tr_recv, "tr")
    tback = tr_recv[0].astype(F32)
    for hd in range(1, 8):
        tback = tback + tr_recv[hd].astype(F32)
    tdn_all[x] = ((1.0 + l_tmod[1:2, quarter]) * tback).astype(BF16)
    for t in (2, 1, 3):
        remote(tdn_all.at[x], tdn_all.at[x], "tdn", dev(dx=(x + t) % 4)).start()
    expect("tdn", tdn_all.at[pl.ds(0, 3)])
    leave(tdn_all.at[pl.ds(0, 3)], "tdn")
    got(s2_buf.at[pl.ds(0, 3)], "s2")
    s3_buf[c] = s2_buf[0] + s2_buf[1] + s2_buf[2] + s2_buf[3]
    remote(s3_buf.at[c], s3_buf.at[c], "s3", dev(dc=1 - c)).start()
    expect("s3", s3_buf.at[0])
    leave(s3_buf.at[0], "s3")

    for ch in range(3):
        lane_cols = slice(128 * ch, 128 * ch + 128)
        total = wt[pos, :, lane_cols]
        for way in range(2):
            got(ring_r.at[way, 3, ch], "r%d3%d" % (way, ch))
            total = total + ring_r[way, 3, ch].astype(F32)
        fin_s[0, ch] = total[0:96, :].astype(BF16)
        fin_s[1, ch] = total[96:192, :].astype(BF16)
    for n in range(2):
        own = jnp.logical_and(c == mine, n == half)

        @pl.when(jnp.logical_not(own))
        def _():
            remote(fin_s.at[n], fin_r.at[half], "fin", dev(dx=2 * c + n, dc=mine)).start()

        @pl.when(own)
        def _():
            local(fin_s.at[n], fin_r.at[half], "fin").start()
    expect("fin", fin_r)
    leave_if(c == mine, fin_s.at[0], "fin")
    leave_if(c != mine, fin_s, "fin")

    def write(n, src):
        pltpu.make_async_copy(src, results[n], os_.at[n]).start()

    got(s3_buf.at[0], "s3")
    for m in range(8):
        o_vs[:, 384 * m:384 * m + 384] = jnp.concatenate(
            [s3_buf[core, :, 192 * m:192 * m + 192] for core in range(2)], axis=1)
    write(4, o_vs)
    got(tsx_buf.at[pl.ds(0, 3)], "tsx")
    for xx in range(4):
        o_ts[:, 768 * xx:768 * xx + 768] = tsx_buf[xx]
    write(5, o_ts)
    got(y_recv.at[pl.ds(0, 3)], "by")
    back = b_own[rows32(y), :]
    for yy in range(4):
        back = back + jnp.where(yy == y, 0.0, y_recv[yy].astype(F32))
    o_dn[...] = ((1.0 + l_mod[1:2, :]) * back).astype(BF16)
    write(0, o_dn)
    got(tw_r, "tw")
    o_twg[...] += tw_r[...].astype(F32)
    write(3, o_twg)
    got(tdn_all.at[pl.ds(0, 3)], "tdn")
    for xx in range(4):
        o_tdn[:, 768 * xx:768 * xx + 768] = tdn_all[xx]
    write(1, o_tdn)
    got(fin_r, "fin")
    for ch in range(3):
        for j in range(2):
            o_wg[ch, :, 128 * j:128 * j + 128] = fin_r[j, ch].astype(F32)
    write(2, o_wg)
    for n, src in enumerate((o_dn, o_tdn, o_wg, o_twg, o_vs, o_ts)):
        pltpu.make_async_copy(src, results[n], os_.at[n]).wait()


def finish(*refs):
    into = [pltpu.make_async_copy(refs[n], refs[12 + n], refs[18].at[n]) for n in range(6)]
    back = [pltpu.make_async_copy(refs[12 + n], refs[6 + n], refs[18].at[n]) for n in range(6)]
    for copy in into:
        copy.start()
    for first, second in zip(into, back):
        first.wait()
        second.start()
    for copy in back:
        copy.wait()


SCRATCH = (
    ((32, D), BF16), ((32, D), BF16), ((3, 96, 256), F32), ((3, 96, 256), F32), ((2, D), F32), ((2, D), F32),
    ((32, 2048), BF16), ((32, 2048), BF16), ((32, 2048), BF16), ((32, 2048), BF16),
    ((32, D), BF16), ((32, D), BF16), ((3, D, 256), BF16), ((3, 768, 256), BF16),
    ((2, 256), F32), ((2, 256), F32), ((2, D), F32), ((2, D), F32),
    ((4, 2, ROWS, 128), BF16), ((2, 2, ROWS, 128), BF16), ((4, 16, 128), F32),
    ((16, 8, 128), F32), ((16, 8, 128), F32), ((2, 2, 8, 128), F32), ((4, 8, 128), F32),
    ((2, ROWS, 128), F32), ((2, ROWS, 128), F32), ((4, ROWS, 128), F32),
    ((2, ROWS, 128), BF16), ((2, ROWS, 128), BF16), ((2, ROWS, 128), BF16), ((2, ROWS, 128), BF16),
    ((ROWS, 128), BF16), ((ROWS, 128), BF16), ((2, 4, 4, 32, 384), BF16), ((3, 32, 128), BF16),
    ((2, 32, 1536), BF16), ((2, 4, 4, 32, 1536), BF16), ((3, 1536, 128), BF16),
    ((1536, 128), F32), ((1536, 128), F32), ((1536, 384), F32), ((2, 1536, 128), F32), ((32, D), BF16), ((256, 512), BF16), ((256, 768), BF16),
    ((3, 4, 32, 128), BF16), ((3, 4, 2, 32, 256), BF16), ((2, 4, 32, 768), BF16),
    ((8, 192, 384), F32), ((2, 4, 3, 192, 128), BF16), ((2, 4, 3, 192, 128), BF16),
    ((2, 3, 96, 128), BF16), ((2, 3, 96, 128), BF16),
    ((128, D), BF16), ((128, D), BF16), ((128, D), F32), ((4, 32, D), BF16), ((4, 32, D), BF16),
    ((512, 256), BF16), ((8, 32, 768), BF16), ((8, 32, 768), BF16), ((4, 32, 768), BF16), ((8, 2, 768), F32), ((4, 2, 768), F32),
    ((16, 2, 1536), F32), ((4, 2, 1536), F32), ((2, 2, 1536), F32),
    ((3, 96, 256), BF16), ((3, 96, 256), BF16),
)


def body(
    video_q, video_k, video_v, video_out, video_dout, text_q, text_k, text_v, text_out, text_dout,
    video_lse, text_lse, video_norm, text_norm, video_mod, text_mod, video_weight, text_weight,
):
    args = [a[0] for a in (
        video_q, video_k, video_v, video_out, video_dout, text_q, text_k, text_v, text_out, text_dout,
        video_lse, text_lse, video_norm, text_norm, video_mod, text_mod)]
    args += [jnp.transpose(w, (1, 0, 2)) for w in (video_weight, text_weight)]
    results = pl.pallas_call(
        kernel,
        out_shape=(
            jax.ShapeDtypeStruct((32, D), BF16), jax.ShapeDtypeStruct((32, D), BF16),
            jax.ShapeDtypeStruct((3, 96, 256), F32), jax.ShapeDtypeStruct((3, 96, 256), F32),
            jax.ShapeDtypeStruct((2, D), F32), jax.ShapeDtypeStruct((2, D), F32),
        ),
        in_specs=[pl.BlockSpec(memory_space=pl.ANY)] * len(args),
        out_specs=[pl.BlockSpec(memory_space=pl.ANY)] * 6,
        scratch_shapes=[pltpu.VMEM(shape, kind) for shape, kind in SCRATCH] + [
            pltpu.SemaphoreType.DMA((len(NAMES),)),
            pltpu.SemaphoreType.DMA((len(NAMES),)),
            pltpu.SemaphoreType.DMA((len(LOCALS),)),
            pltpu.SemaphoreType.DMA((6,)),
        ],
        compiler_params=pltpu.CompilerParams(collective_id=0, has_side_effects=True, vmem_limit_bytes=60 * 1024 * 1024),
    )(*args)
    anywhere = pl.BlockSpec(memory_space=pl.ANY)
    dn, tdn, wg, twg, vs, ts = pl.pallas_call(
        finish,
        out_shape=[jax.ShapeDtypeStruct(r.shape, r.dtype) for r in results],
        in_specs=[anywhere] * 6,
        out_specs=[anywhere] * 6,
        scratch_shapes=[pltpu.VMEM(r.shape, r.dtype) for r in results] + [pltpu.SemaphoreType.DMA((6,))],
        compiler_params=pltpu.CompilerParams(vmem_limit_bytes=60 * 1024 * 1024),
    )(*results)
    return (
        dn[None], tdn[None], jnp.transpose(wg, (1, 0, 2)), jnp.transpose(twg, (1, 0, 2)), vs[None], ts[None],
    )


def solution(mesh):
    tokens = P("dp", ("blk", "head"), None)
    text = P("dp", "head", None)
    whole = P("dp", None, None)
    columns = P(None, None, "head")
    return jax.shard_map(
        body,
        mesh=mesh,
        in_specs=(tokens,) * 5 + (text,) * 5 + (
            P("dp", "head", "blk"), P("dp", "head", None), tokens, text, whole, whole, columns, columns),
        out_specs=(
            tokens, text, P(("dp", "blk"), None, "head"), P(("dp", "blk"), None, "head"), whole, whole),
        check_vma=False,
    )
```

time: 99.3 us -> 85.8 us (0.86)
  Pallas kernels: 98.5 us -> 84.9 us
    pallas_call x1, Pallas kernels: 96.5 us -> 82.9 us  [body(): pl.pallas_call(kernel, out_shape=(jax.ShapeDtypeStruct((32, D), BF16), ja...]
where the time goes in v3:
time: 85.8 us; the launch traced here: 85.7 us
  Pallas kernels  84.9 us (99%)
    pallas_call x1, Pallas kernels, body(): pl.pallas_call(kernel, out_shape=(jax.ShapeDtypeStruct((32, D), BF16), ja...  82.9 us
    pallas_call x1, Pallas kernels, body(): pl.pallas_call(finish, out_shape=[jax.ShapeDtypeStruct(r.shape, r.dtype)...  2.03 us

profile of v3, /device:TPU:1, one launch (start us, length us, event | category | flops | bytes accessed | tf_op | source)
XLA Modules:
  0.0 85.7 jit_solution(6362320234924070448)
XLA Ops:
  0.6 82.9 %shard_map.217 = (bf16[32,3072]{1,0:T(8,128)(2,1)}, bf16[32,3072]{1,0:T(8,128)(2,1)}, f32[3,96,256]{2,1,0:T(8,128)}, f32[3,96,256]{2,1,0:T(8,128)}, f32[2,3072]{1,0:T(2,128)}, /*index=5*/f32[2,3072]{1,0:T(2,128)}) custom-call(bf16[32,2048]{1,0:T(8,128)(2,1)} %bitcast.28, bf16[32,2048]{1,0:T(8,128)(2,1)} %bitcast.29, bf16[32,2048]{1,0:T(8,128)(2,1)} %bitcast.30, ...), custom_call_target="tpu_custom_call" | custom-call | tf_op jit(solution)/shard_map/pallas_call | solution.py:850
  83.5 2.0 %shard_map.218 = (bf16[32,3072]{1,0:T(8,128)(2,1)}, bf16[32,3072]{1,0:T(8,128)(2,1)}, f32[3,96,256]{2,1,0:T(8,128)}, f32[3,96,256]{2,1,0:T(8,128)}, f32[2,3072]{1,0:T(2,128)}, /*index=5*/f32[2,3072]{1,0:T(2,128)}) custom-call(bf16[32,3072]{1,0:T(8,128)(2,1)} %get-tuple-element.18.refs_0_, bf16[32,3072]{1,0:T(8,128)(2,1)} %get-tuple-element.19.refs_1_, ...), custom_call_target="tpu_custom_call" | custom-call | tf_op jit(solution)/shard_map/pallas_call | solution.py:868

commit v4 on v3

--- a/solution.py
+++ b/solution.py
@@ -20,9 +20,9 @@
 
 NAMES = (
     "a_q", "a_d", "a_k", "a_v", "a_st", "a_lse", "a_tq", "a_td", "a_tk", "a_tv",
-    "b_kv", "b_qc", "b_sc", "b_qz", "b_sz", "b_qf", "b_sf", "v0", "wq", "tin", "tq",
-    "d_kv", "d_qc", "d_qz", "gkv", "gq", "e", "tz", "te",
-    "bc0", "bc1", "bc2", "bc3", "bc4", "bc5", "by", "tr", "tdn", "ts", "tsx", "s1", "s2", "s3", "tw", "fin",
+    "b_kv", "b_qc", "b_sc", "b_qz", "b_sz", "b_qf", "b_sf", "v0", "wq", "tin",
+    "d_kv", "d_qc", "d_qz", "gkv", "gq", "e", "tz", "tzs", "te",
+    "bc0", "bc1", "bc2", "bc3", "bc4", "bc5", "by", "tr", "tdz", "tdn", "ts", "ts2", "tsx", "s1", "s2", "s3", "tx", "tf", "fin",
 )
 RING = tuple("r%d%d%d" % (way, step, ch) for way in range(2) for step in range(4) for ch in range(3))
 INPUTS = tuple("v1%d%d" % (t, n) for t in (1, 2, 3) for n in range(4)) + tuple("v2%d" % n for n in range(4))
@@ -57,9 +57,9 @@
     l_out, l_dout, l_tout, l_tdout, l_nrm, l_tnrm, l_w, l_tw, l_lse, l_tlse, l_mod, l_tmod,
     qd, kv, st, d_send, d_recv, l_send, l_recv,
     gk_acc, gv_acc, gq_acc, dkv_s, dkv_r, dqc_s, dqc_r, dqz_s, dqz_r, gw, g_txt,
-    vin_s, vin_all, wq, gain_col, shift_col, m_acc, s_acc, tin_s, tin_all, tq_all, tz, tg, gs,
+    vin_s, vin_all, wq, gain_col, shift_col, m_acc, s_acc, tin_s, tin_x, tin_all, tzz, tgz, gs,
     wt, ring_s, ring_r, fin_s, fin_r, b_send, b_recv, b_own, y_send, y_recv,
-    t_tmp, tr_send, tr_recv, tdn_all, ts_buf, tsx_buf, s1_buf, s2_buf, s3_buf, tw_s, tw_r,
+    tr_send, tr_recv, tdn_all, ts_buf, ts2_buf, tsx_buf, s1_buf, s2_buf, s3_buf, tw_s, tf_s, tf_r,
     rs, ss, ls, os_,
 ):
     results = (r_dn, r_tdn, r_wg, r_twg, r_vs, r_ts)
@@ -306,6 +306,13 @@
     ready("tmod")
     tgain = 1.0 + l_tmod[1:2, :]
     tin_s[...] = (tgain * l_tnrm[...].astype(F32) + l_tmod[0:1, :]).astype(BF16)
+
+    def text_cols(clip):
+        return tin_s.at[:, pl.ds(pl.multiple_of(clip * 1536 + z * 384, 128), 384)]
+
+    remote(text_cols(1 - dp), tin_x, "tx", dev(ddp=1 - dp)).start()
+    expect("tx", tin_x)
+    leave(tin_x, "tx")
 
     along = jnp.where(c == 0, y, x)
 
@@ -386,31 +393,17 @@
         expect("v2%d" % n, every)
         leave(every, "v2%d" % n)
 
-    window = jnp.minimum((blk * 96) // 128 * 128, 1280)
-
     peers = [(j, m) for j in (2, 1, 3, 0) for m in (0, 1) if (j, m) != (0, 0)]
     quarter = pl.ds(pl.multiple_of(x * 768, 768), 768)
 
-    def to_peers(copies_for, name):
+    got(tin_x, "tx")
+    for src, clip in ((text_cols(dp), dp), (tin_x, 1 - dp)):
+        place = tin_all.at[clip, c, y]
+        local(src, place, "tin").start()
         for j, m in peers:
-            yy, cc = (y + j) % 4, (c + m) % 2
-            for src, dst in copies_for(yy * 2 + cc):
-                remote(src, dst, name, dev(dy=yy, dc=cc)).start()
-
-    def tin_copies(hd):
-        return [(tin_s.at[:, pl.ds(pl.multiple_of(other * 1536 + window, 128), 256)],
-                 tin_all.at[rows32(head), pl.ds(other * 256, 256)]) for other in range(2)]
-
-    for src, dst in tin_copies(head):
-        local(src, dst, "tin").start()
-    to_peers(tin_copies, "tin")
-    place = tq_all.at[rows32(head)]
-    local(l_tnrm.at[:, quarter], place, "tq").start()
-    to_peers(lambda hd: [(l_tnrm.at[:, quarter], place)], "tq")
-    expect("tq", tq_all)
-    leave(tq_all.at[pl.ds(0, 7 * 32)], "tq")
+            remote(src, place, "tin", dev(dy=(y + j) % 4, dc=(c + m) % 2)).start()
     expect("tin", tin_all)
-    leave(tin_all.at[pl.ds(0, 7 * 32)], "tin")
+    leave(tr_recv.at[pl.ds(0, 7), :, pl.ds(0, 768)], "tin")
 
     def pair(lse_row, delta_row, query, dquery, keys, values):
         probs = jnp.exp2(nt(keys, query) * (FACTOR * LOG2E) - lse_row)
@@ -521,7 +514,7 @@
 
     def finish_channel(ch, value):
         gw[c, :, :, :, 128 * ch:128 * ch + 128] = value[0:SET, :].reshape(4, 4, 32, 128)
-        g_txt[ch] = value[SET:ROWS, :]
+        g_txt[:, 128 * ch:128 * ch + 128] = value[SET:ROWS, :]
 
     got(dkv_r, "d_kv")
     finish_channel(1, (gk_acc[0] * FACTOR + dkv_r[0].astype(F32)).astype(BF16))
@@ -535,16 +528,27 @@
         one = gw.at[0, :, 0, :, pl.ds(128 * ch, 128)]
         leave_if(c == mine, one, "e", 3)
         leave_if(c != mine, one, "e", 4)
-    for zz in range(4):
-        @pl.when(z != zz)
-        def _():
-            remote(g_txt, tz.at[:, z], "tz", dev(dz=zz)).start()
-
-        @pl.when(z == zz)
-        def _():
-            local(g_txt, tz.at[:, z], "tz").start()
-    expect("tz", tz)
-    leave(tz.at[:, pl.ds(0, 3)], "tz")
+    for xx in (2, 1, 3, 0):
+        own = jnp.logical_and(xx == 0, c == mine)
+        for ch in range(3):
+            piece = g_txt.at[:, pl.ds(128 * ch, 128)]
+            place = tgz.at[c, :, pl.ds(pl.multiple_of(256 * ch + 128 * half, 128), 128)]
+
+            @pl.when(jnp.logical_not(own))
+            def _():
+                remote(piece, place, "te", dev(dx=(x + xx) % 4, dc=mine)).start()
+
+            @pl.when(own)
+            def _():
+                local(piece, place, "te").start()
+    expect("te", tgz)
+    leave_if(c == mine, g_txt, "te", 3)
+    leave_if(c != mine, g_txt, "te", 4)
+    local(g_txt, tzz.at[dp, c, z], "tz").start()
+    for t in (4, 3, 5, 2, 6, 1, 7):
+        remote(g_txt, tzz.at[dp, c, z], "tz", along_z(t)).start()
+    expect("tz", tzz.at[:, c])
+    leave(tr_recv.at[pl.ds(0, 7), :, pl.ds(0, 384)], "tz")
 
     got(gw.at[1 - c, :, :, :, pl.ds(128, 256)], "gkv")
     got(gw.at[1 - c, :, :, :, pl.ds(0, 128)], "gq")
@@ -593,24 +597,39 @@
                 expect(name, ring_r.at[way, step, ch, pl.ds(0, size)])
                 leave(out_ref, name)
 
+    def back_chunk(n):
+        cols = slice(512 * n, 512 * n + 512)
+        rows = gs[...].reshape(256, 768)
+        term = (nt(rows[:, 0:256], l_w[0, cols, :]) + nt(rows[:, 256:512], l_w[1, cols, :])
+                + nt(rows[:, 512:768], l_w[2, cols, :]))
+
+        @pl.when(c == 0)
+        def _():
+            b_own[:, cols] = term[0:128, :]
+            b_send[:, cols] = term[128:256, :].astype(BF16)
+
+        @pl.when(c == 1)
+        def _():
+            b_own[:, cols] = term[128:256, :]
+            b_send[:, cols] = term[0:128, :].astype(BF16)
+        remote(b_send.at[:, cols], b_recv.at[:, cols], "bc%d" % n, dev(dc=1 - c)).start()
+        expect("bc%d" % n, b_recv.at[:, cols])
+        leave(b_send.at[:, cols], "bc%d" % n)
+
+    def gather_chunk(n):
+        cols = slice(512 * n, 512 * n + 512)
+        got(b_recv.at[:, cols], "bc%d" % n)
+        total = b_own[:, cols] + b_recv[:, cols].astype(F32)
+        b_own[:, cols] = total
+        for yy in range(4):
+            y_send[yy, :, cols] = total[32 * yy:32 * yy + 32, :].astype(BF16)
+
+            @pl.when(yy != y)
+            def _():
+                remote(y_send.at[yy, :, cols], y_recv.at[y, :, cols], "by", dev(dy=yy)).start()
+
     project(0)
     ring(0)
-    got(tz, "tz")
-    for xx in (2, 1, 3, 0):
-        to = (x + xx) % 4
-        own = jnp.logical_and(xx == 0, c == mine)
-        place = tg.at[:, :, c, :, lanes(half)]
-
-        @pl.when(jnp.logical_not(own))
-        def _():
-            remote(tz, place, "te", dev(dx=to, dc=mine)).start()
-
-        @pl.when(own)
-        def _():
-            local(tz, place, "te").start()
-    expect("te", tg)
-    leave_if(c == mine, tz, "te", 3)
-    leave_if(c != mine, tz, "te", 4)
     project(1)
     project(2)
     project(3)
@@ -635,85 +654,58 @@
         remote(s1_buf.at[me], s1_buf.at[me], "s1", dev(dx=chip(i, j)[0], dy=chip(i, j)[1])).start()
     expect("s1", s1_buf.at[pl.ds(0, 15)])
     leave(s1_buf.at[pl.ds(0, 15)], "s1")
+    got(tgz, "te")
+    ready("tw")
+    rows = tgz[...].reshape(64, 768)
+    term = (nt(rows[:, 0:256], l_tw[0]) + nt(rows[:, 256:512], l_tw[1]) + nt(rows[:, 512:768], l_tw[2]))
+    for core in range(2):
+        tr_send[core] = term[32 * core:32 * core + 32, :].astype(BF16)
+        own = jnp.logical_and(y == z, c == core)
+
+        @pl.when(jnp.logical_not(own))
+        def _():
+            remote(tr_send.at[core], tr_recv.at[head], "tr", dev(dy=z, dc=core)).start()
+
+        @pl.when(own)
+        def _():
+            local(tr_send.at[core], tr_recv.at[head], "tr").start()
+    leave_if(y == z, tr_send.at[0], "tr")
+    leave_if(y != z, tr_send, "tr")
+
     ring(1)
-
-    def back_chunk(n):
-        cols = slice(512 * n, 512 * n + 512)
-        rows = gs[...].reshape(256, 768)
-        term = (nt(rows[:, 0:256], l_w[0, cols, :]) + nt(rows[:, 256:512], l_w[1, cols, :])
-                + nt(rows[:, 512:768], l_w[2, cols, :]))
-
-        @pl.when(c == 0)
-        def _():
-            b_own[:, cols] = term[0:128, :]
-            b_send[:, cols] = term[128:256, :].astype(BF16)
-
-        @pl.when(c == 1)
-        def _():
-            b_own[:, cols] = term[128:256, :]
-            b_send[:, cols] = term[0:128, :].astype(BF16)
-        remote(b_send.at[:, cols], b_recv.at[:, cols], "bc%d" % n, dev(dc=1 - c)).start()
-        expect("bc%d" % n, b_recv.at[:, cols])
-        leave(b_send.at[:, cols], "bc%d" % n)
-
-    def gather_chunk(n):
-        cols = slice(512 * n, 512 * n + 512)
-        got(b_recv.at[:, cols], "bc%d" % n)
-        total = b_own[:, cols] + b_recv[:, cols].astype(F32)
-        b_own[:, cols] = total
-        for yy in range(4):
-            y_send[yy, :, cols] = total[32 * yy:32 * yy + 32, :].astype(BF16)
-
-            @pl.when(yy != y)
-            def _():
-                remote(y_send.at[yy, :, cols], y_recv.at[y, :, cols], "by", dev(dy=yy)).start()
-
     ready("w")
     got(gs, "e")
-    back_chunk(0)
-    back_chunk(1)
-    gather_chunk(0)
-    back_chunk(2)
-    gather_chunk(1)
-    back_chunk(3)
-    gather_chunk(2)
-    back_chunk(4)
-    gather_chunk(3)
-    back_chunk(5)
-    gather_chunk(4)
-    gather_chunk(5)
+    for n in range(6):
+        back_chunk(n)
+
+    for n in range(6):
+        gather_chunk(n)
     expect("by", y_recv.at[pl.ds(0, 3)])
     leave(y_send.at[pl.ds(0, 3)], "by")
+
+    @pl.when(y == z)
+    def _():
+        got(tr_recv, "tr")
+        tback = tr_recv[0].astype(F32)
+        for hd in range(1, 8):
+            tback = tback + tr_recv[hd].astype(F32)
+        tdn_all[x] = ((1.0 + l_tmod[1:2, quarter]) * tback).astype(BF16)
+        for t in (2, 1, 3):
+            remote(tdn_all.at[x], tdn_all.at[x], "tdz", dev(dz=(z + t) % 4)).start()
+        ts_buf[c] = jnp.concatenate([
+            jnp.sum(tback, axis=0, keepdims=True),
+            jnp.sum(tback * l_tnrm[:, quarter].astype(F32), axis=0, keepdims=True)], axis=0)
+        for j, m in peers:
+            remote(ts_buf.at[c], ts_buf.at[c], "ts", dev(dy=(y + j) % 4, dc=(c + m) % 2)).start()
+    leave_if(y == z, tdn_all.at[pl.ds(0, 3)], "tdz")
+    for _ in range(7):
+        leave_if(y == z, ts_buf.at[0], "ts")
+
     ring(2)
-
-    got(tg, "te")
-    ready("tw")
-    term = (nt(tg[0].reshape(256, 256), l_tw[0]) + nt(tg[1].reshape(256, 256), l_tw[1])
-            + nt(tg[2].reshape(256, 256), l_tw[2]))
-    for hd in range(8):
-        tr_send[hd] = term[32 * hd:32 * hd + 32, :].astype(BF16)
-    local(tr_send.at[head], tr_recv.at[head], "tr").start()
-    to_peers(lambda hd: [(tr_send.at[hd], tr_recv.at[head])], "tr")
-    expect("tr", tr_recv)
-    leave(tr_recv.at[pl.ds(0, 7)], "tr")
-    got(tq_all, "tq")
-    ts_buf[head] = jnp.concatenate([jnp.sum(term, axis=0, keepdims=True),
-                                    jnp.sum(term * tq_all[...].astype(F32), axis=0, keepdims=True)], axis=0)
-    to_peers(lambda hd: [(ts_buf.at[head], ts_buf.at[head])], "ts")
-    expect("ts", ts_buf.at[pl.ds(0, 7)])
-    leave(ts_buf.at[pl.ds(0, 7)], "ts")
-
-    got(tin_all, "tin")
-    first = pl.multiple_of(blk * 96 - window, 32)
-    away = pl.multiple_of((1 - dp) * 256 + first, 32)
-    near = pl.multiple_of(dp * 256 + first, 32)
-    for ch in range(3):
-        t_tmp[...] = tn(tin_all[...], tg[ch].reshape(256, 256)).astype(BF16)
-        tw_s[ch] = t_tmp[pl.ds(away, 96), :]
-        o_twg[ch] = t_tmp[pl.ds(near, 96), :].astype(F32)
-    remote(tw_s, tw_r, "tw", dev(ddp=1 - dp)).start()
-    expect("tw", tw_r)
-    leave(tw_s, "tw")
+    got(tzz.at[:, c], "tz")
+    remote(tzz.at[:, c], tzz.at[:, c], "tzs", dev(dc=1 - c)).start()
+    expect("tzs", tzz.at[:, 1 - c])
+    leave(tzz.at[:, c], "tzs")
 
     got(s1_buf.at[pl.ds(0, 15)], "s1")
     stat = s1_buf[0]
@@ -725,29 +717,43 @@
     expect("s2", s2_buf.at[pl.ds(0, 3)])
     leave(s2_buf.at[pl.ds(0, 3)], "s2")
     ring(3)
-    got(ts_buf.at[pl.ds(0, 7)], "ts")
-    tstat = ts_buf[0]
-    for hd in range(1, 8):
-        tstat = tstat + ts_buf[hd]
-    tsx_buf[x] = tstat
-    for t in (2, 1, 3):
-        remote(tsx_buf.at[x], tsx_buf.at[x], "tsx", dev(dx=(x + t) % 4)).start()
-    expect("tsx", tsx_buf.at[pl.ds(0, 3)])
-    leave(tsx_buf.at[pl.ds(0, 3)], "tsx")
-    got(tr_recv, "tr")
-    tback = tr_recv[0].astype(F32)
-    for hd in range(1, 8):
-        tback = tback + tr_recv[hd].astype(F32)
-    tdn_all[x] = ((1.0 + l_tmod[1:2, quarter]) * tback).astype(BF16)
+    @pl.when(y == z)
+    def _():
+        got(ts_buf.at[0], "ts")
+
+    @pl.when(y != z)
+    def _():
+        got(ts_buf, "ts")
+        got(tdn_all.at[x], "tdz")
     for t in (2, 1, 3):
         remote(tdn_all.at[x], tdn_all.at[x], "tdn", dev(dx=(x + t) % 4)).start()
     expect("tdn", tdn_all.at[pl.ds(0, 3)])
     leave(tdn_all.at[pl.ds(0, 3)], "tdn")
-    got(s2_buf.at[pl.ds(0, 3)], "s2")
-    s3_buf[c] = s2_buf[0] + s2_buf[1] + s2_buf[2] + s2_buf[3]
-    remote(s3_buf.at[c], s3_buf.at[c], "s3", dev(dc=1 - c)).start()
-    expect("s3", s3_buf.at[0])
-    leave(s3_buf.at[0], "s3")
+    ts2_buf[z] = ts_buf[0] + ts_buf[1]
+    for t in (2, 1, 3):
+        remote(ts2_buf.at[z], ts2_buf.at[z], "ts2", dev(dz=(z + t) % 4)).start()
+    expect("ts2", ts2_buf.at[pl.ds(0, 3)])
+    leave(ts2_buf.at[pl.ds(0, 3)], "ts2")
+
+    got(tzz.at[:, 1 - c], "tzs")
+    got(tin_all, "tin")
+    tw_s[...] = tn(tin_all[...].reshape(512, 384), tzz[...].reshape(512, 384)).astype(BF16)
+    for n in range(2):
+        for ch in range(3):
+            rows = pl.ds(pl.multiple_of(192 * c + 96 * n, 32), 96)
+            tf_s[n, ch] = tw_s[rows, 128 * ch:128 * ch + 128]
+        own = jnp.logical_and(c == mine, n == half)
+
+        @pl.when(jnp.logical_not(own))
+        def _():
+            remote(tf_s.at[n], tf_r.at[half], "tf", dev(dx=2 * c + n, dc=mine)).start()
+
+        @pl.when(own)
+        def _():
+            local(tf_s.at[n], tf_r.at[half], "tf").start()
+    expect("tf", tf_r)
+    leave_if(c == mine, tf_s.at[0], "tf")
+    leave_if(c != mine, tf_s, "tf")
 
     for ch in range(3):
         lane_cols = slice(128 * ch, 128 * ch + 128)
@@ -771,6 +777,19 @@
     leave_if(c == mine, fin_s.at[0], "fin")
     leave_if(c != mine, fin_s, "fin")
 
+    got(s2_buf.at[pl.ds(0, 3)], "s2")
+    s3_buf[c] = s2_buf[0] + s2_buf[1] + s2_buf[2] + s2_buf[3]
+    remote(s3_buf.at[c], s3_buf.at[c], "s3", dev(dc=1 - c)).start()
+    expect("s3", s3_buf.at[0])
+    leave(s3_buf.at[0], "s3")
+
+    got(ts2_buf.at[pl.ds(0, 3)], "ts2")
+    tsx_buf[x] = ts2_buf[0] + ts2_buf[1] + ts2_buf[2] + ts2_buf[3]
+    for t in (2, 1, 3):
+        remote(tsx_buf.at[x], tsx_buf.at[x], "tsx", dev(dx=(x + t) % 4)).start()
+    expect("tsx", tsx_buf.at[pl.ds(0, 3)])
+    leave(tsx_buf.at[pl.ds(0, 3)], "tsx")
+
     def write(n, src):
         pltpu.make_async_copy(src, results[n], os_.at[n]).start()
 
@@ -779,28 +798,30 @@
         o_vs[:, 384 * m:384 * m + 384] = jnp.concatenate(
             [s3_buf[core, :, 192 * m:192 * m + 192] for core in range(2)], axis=1)
     write(4, o_vs)
-    got(tsx_buf.at[pl.ds(0, 3)], "tsx")
-    for xx in range(4):
-        o_ts[:, 768 * xx:768 * xx + 768] = tsx_buf[xx]
-    write(5, o_ts)
     got(y_recv.at[pl.ds(0, 3)], "by")
     back = b_own[rows32(y), :]
     for yy in range(4):
         back = back + jnp.where(yy == y, 0.0, y_recv[yy].astype(F32))
     o_dn[...] = ((1.0 + l_mod[1:2, :]) * back).astype(BF16)
     write(0, o_dn)
-    got(tw_r, "tw")
-    o_twg[...] += tw_r[...].astype(F32)
-    write(3, o_twg)
     got(tdn_all.at[pl.ds(0, 3)], "tdn")
     for xx in range(4):
         o_tdn[:, 768 * xx:768 * xx + 768] = tdn_all[xx]
     write(1, o_tdn)
+    got(tsx_buf.at[pl.ds(0, 3)], "tsx")
+    for xx in range(4):
+        o_ts[:, 768 * xx:768 * xx + 768] = tsx_buf[xx]
+    write(5, o_ts)
     got(fin_r, "fin")
     for ch in range(3):
         for j in range(2):
             o_wg[ch, :, 128 * j:128 * j + 128] = fin_r[j, ch].astype(F32)
     write(2, o_wg)
+    got(tf_r, "tf")
+    for ch in range(3):
+        for j in range(2):
+            o_twg[ch, :, 128 * j:128 * j + 128] = tf_r[j, ch].astype(F32)
+    write(3, o_twg)
     for n, src in enumerate((o_dn, o_tdn, o_wg, o_twg, o_vs, o_ts)):
         pltpu.make_async_copy(src, results[n], os_.at[n]).wait()
 
@@ -826,16 +847,16 @@
     ((16, 8, 128), F32), ((16, 8, 128), F32), ((2, 2, 8, 128), F32), ((4, 8, 128), F32),
     ((2, ROWS, 128), F32), ((2, ROWS, 128), F32), ((4, ROWS, 128), F32),
     ((2, ROWS, 128), BF16), ((2, ROWS, 128), BF16), ((2, ROWS, 128), BF16), ((2, ROWS, 128), BF16),
-    ((ROWS, 128), BF16), ((ROWS, 128), BF16), ((2, 4, 4, 32, 384), BF16), ((3, 32, 128), BF16),
+    ((ROWS, 128), BF16), ((ROWS, 128), BF16), ((2, 4, 4, 32, 384), BF16), ((32, 384), BF16),
     ((2, 32, 1536), BF16), ((2, 4, 4, 32, 1536), BF16), ((3, 1536, 128), BF16),
-    ((1536, 128), F32), ((1536, 128), F32), ((1536, 384), F32), ((2, 1536, 128), F32), ((32, D), BF16), ((256, 512), BF16), ((256, 768), BF16),
-    ((3, 4, 32, 128), BF16), ((3, 4, 2, 32, 256), BF16), ((2, 4, 32, 768), BF16),
+    ((1536, 128), F32), ((1536, 128), F32), ((1536, 384), F32), ((2, 1536, 128), F32), ((32, D), BF16), ((32, 384), BF16), ((2, 2, 4, 32, 384), BF16),
+    ((2, 2, 4, 32, 384), BF16), ((2, 32, 768), BF16), ((2, 4, 32, 768), BF16),
     ((8, 192, 384), F32), ((2, 4, 3, 192, 128), BF16), ((2, 4, 3, 192, 128), BF16),
     ((2, 3, 96, 128), BF16), ((2, 3, 96, 128), BF16),
     ((128, D), BF16), ((128, D), BF16), ((128, D), F32), ((4, 32, D), BF16), ((4, 32, D), BF16),
-    ((512, 256), BF16), ((8, 32, 768), BF16), ((8, 32, 768), BF16), ((4, 32, 768), BF16), ((8, 2, 768), F32), ((4, 2, 768), F32),
+    ((2, 32, 768), BF16), ((8, 32, 768), BF16), ((4, 32, 768), BF16), ((2, 2, 768), F32), ((4, 2, 768), F32), ((4, 2, 768), F32),
     ((16, 2, 1536), F32), ((4, 2, 1536), F32), ((2, 2, 1536), F32),
-    ((3, 96, 256), BF16), ((3, 96, 256), BF16),
+    ((384, 384), BF16), ((2, 3, 96, 128), BF16), ((2, 3, 96, 128), BF16),
 )
 
 

time: 85.8 us -> 81.7 us (0.952)
  Pallas kernels: 84.9 us -> 80.7 us
    pallas_call x1, Pallas kernels: 82.9 us -> 78.7 us  [body(): pl.pallas_call(kernel, out_shape=(jax.ShapeDtypeStruct((32, D), BF16), ja...]
where the time goes in v4:
time: 81.7 us; the launch traced here: 81.4 us
  Pallas kernels  80.7 us (99%)
    pallas_call x1, Pallas kernels, body(): pl.pallas_call(kernel, out_shape=(jax.ShapeDtypeStruct((32, D), BF16), ja...  78.7 us
    pallas_call x1, Pallas kernels, body(): pl.pallas_call(finish, out_shape=[jax.ShapeDtypeStruct(r.shape, r.dtype)...  2.03 us

profile of v4, /device:TPU:1, one launch (start us, length us, event | category | flops | bytes accessed | tf_op | source)
XLA Modules:
  0.0 81.4 jit_solution(14791375569554217101)
XLA Ops:
  0.6 78.7 %shard_map.217 = (bf16[32,3072]{1,0:T(8,128)(2,1)}, bf16[32,3072]{1,0:T(8,128)(2,1)}, f32[3,96,256]{2,1,0:T(8,128)}, f32[3,96,256]{2,1,0:T(8,128)}, f32[2,3072]{1,0:T(2,128)}, /*index=5*/f32[2,3072]{1,0:T(2,128)}) custom-call(bf16[32,2048]{1,0:T(8,128)(2,1)} %bitcast.28, bf16[32,2048]{1,0:T(8,128)(2,1)} %bitcast.29, bf16[32,2048]{1,0:T(8,128)(2,1)} %bitcast.30, ...), custom_call_target="tpu_custom_call" | custom-call | tf_op jit(solution)/shard_map/pallas_call | solution.py:871
  79.3 2.0 %shard_map.218 = (bf16[32,3072]{1,0:T(8,128)(2,1)}, bf16[32,3072]{1,0:T(8,128)(2,1)}, f32[3,96,256]{2,1,0:T(8,128)}, f32[3,96,256]{2,1,0:T(8,128)}, f32[2,3072]{1,0:T(2,128)}, /*index=5*/f32[2,3072]{1,0:T(2,128)}) custom-call(bf16[32,3072]{1,0:T(8,128)(2,1)} %get-tuple-element.18.refs_0_, bf16[32,3072]{1,0:T(8,128)(2,1)} %get-tuple-element.19.refs_1_, ...), custom_call_target="tpu_custom_call" | custom-call | tf_op jit(solution)/shard_map/pallas_call | solution.py:889

commit v5 on v4

--- a/solution.py
+++ b/solution.py
@@ -678,6 +678,11 @@
     for n in range(6):
         back_chunk(n)
 
+    got(tzz.at[:, c], "tz")
+    remote(tzz.at[:, c], tzz.at[:, c], "tzs", dev(dc=1 - c)).start()
+    expect("tzs", tzz.at[:, 1 - c])
+    leave(tzz.at[:, c], "tzs")
+
     for n in range(6):
         gather_chunk(n)
     expect("by", y_recv.at[pl.ds(0, 3)])
@@ -702,10 +707,25 @@
         leave_if(y == z, ts_buf.at[0], "ts")
 
     ring(2)
-    got(tzz.at[:, c], "tz")
-    remote(tzz.at[:, c], tzz.at[:, c], "tzs", dev(dc=1 - c)).start()
-    expect("tzs", tzz.at[:, 1 - c])
-    leave(tzz.at[:, c], "tzs")
+    got(tzz.at[:, 1 - c], "tzs")
+    got(tin_all, "tin")
+    tw_s[...] = tn(tin_all[...].reshape(512, 384), tzz[...].reshape(512, 384)).astype(BF16)
+    for n in range(2):
+        for ch in range(3):
+            rows = pl.ds(pl.multiple_of(192 * c + 96 * n, 32), 96)
+            tf_s[n, ch] = tw_s[rows, 128 * ch:128 * ch + 128]
+        own = jnp.logical_and(c == mine, n == half)
+
+        @pl.when(jnp.logical_not(own))
+        def _():
+            remote(tf_s.at[n], tf_r.at[half], "tf", dev(dx=2 * c + n, dc=mine)).start()
+
+        @pl.when(own)
+        def _():
+            local(tf_s.at[n], tf_r.at[half], "tf").start()
+    expect("tf", tf_r)
+    leave_if(c == mine, tf_s.at[0], "tf")
+    leave_if(c != mine, tf_s, "tf")
 
     got(s1_buf.at[pl.ds(0, 15)], "s1")
     stat = s1_buf[0]
@@ -734,26 +754,6 @@
         remote(ts2_buf.at[z], ts2_buf.at[z], "ts2", dev(dz=(z + t) % 4)).start()
     expect("ts2", ts2_buf.at[pl.ds(0, 3)])
     leave(ts2_buf.at[pl.ds(0, 3)], "ts2")
-
-    got(tzz.at[:, 1 - c], "tzs")
-    got(tin_all, "tin")
-    tw_s[...] = tn(tin_all[...].reshape(512, 384), tzz[...].reshape(512, 384)).astype(BF16)
-    for n in range(2):
-        for ch in range(3):
-            rows = pl.ds(pl.multiple_of(192 * c + 96 * n, 32), 96)
-            tf_s[n, ch] = tw_s[rows, 128 * ch:128 * ch + 128]
-        own = jnp.logical_and(c == mine, n == half)
-
-        @pl.when(jnp.logical_not(own))
-        def _():
-            remote(tf_s.at[n], tf_r.at[half], "tf", dev(dx=2 * c + n, dc=mine)).start()
-
-        @pl.when(own)
-        def _():
-            local(tf_s.at[n], tf_r.at[half], "tf").start()
-    expect("tf", tf_r)
-    leave_if(c == mine, tf_s.at[0], "tf")
-    leave_if(c != mine, tf_s, "tf")
 
     for ch in range(3):
         lane_cols = slice(128 * ch, 128 * ch + 128)

time: 81.7 us -> 81.5 us (level)
  no operation moved by 1% of the time
where the time goes in v5:
time: 81.5 us; the launch traced here: 81.4 us
  Pallas kernels  80.7 us (99%)
    pallas_call x1, Pallas kernels, body(): pl.pallas_call(kernel, out_shape=(jax.ShapeDtypeStruct((32, D), BF16), ja...  78.7 us
    pallas_call x1, Pallas kernels, body(): pl.pallas_call(finish, out_shape=[jax.ShapeDtypeStruct(r.shape, r.dtype)...  2.03 us

profile of v5, /device:TPU:1, one launch (start us, length us, event | category | flops | bytes accessed | tf_op | source)
XLA Modules:
  0.0 81.4 jit_solution(15831848990289721583)
XLA Ops:
  0.6 78.7 %shard_map.217 = (bf16[32,3072]{1,0:T(8,128)(2,1)}, bf16[32,3072]{1,0:T(8,128)(2,1)}, f32[3,96,256]{2,1,0:T(8,128)}, f32[3,96,256]{2,1,0:T(8,128)}, f32[2,3072]{1,0:T(2,128)}, /*index=5*/f32[2,3072]{1,0:T(2,128)}) custom-call(bf16[32,2048]{1,0:T(8,128)(2,1)} %bitcast.28, bf16[32,2048]{1,0:T(8,128)(2,1)} %bitcast.29, bf16[32,2048]{1,0:T(8,128)(2,1)} %bitcast.30, ...), custom_call_target="tpu_custom_call" | custom-call | tf_op jit(solution)/shard_map/pallas_call | solution.py:871
  79.3 2.0 %shard_map.218 = (bf16[32,3072]{1,0:T(8,128)(2,1)}, bf16[32,3072]{1,0:T(8,128)(2,1)}, f32[3,96,256]{2,1,0:T(8,128)}, f32[3,96,256]{2,1,0:T(8,128)}, f32[2,3072]{1,0:T(2,128)}, /*index=5*/f32[2,3072]{1,0:T(2,128)}) custom-call(bf16[32,3072]{1,0:T(8,128)(2,1)} %get-tuple-element.18.refs_0_, bf16[32,3072]{1,0:T(8,128)(2,1)} %get-tuple-element.19.refs_1_, ...), custom_call_target="tpu_custom_call" | custom-call | tf_op jit(solution)/shard_map/pallas_call | solution.py:889
